TPU v7x, 32 devices: a whole 2x2x4 slice. The times are simulated.
32 devices in a mesh: row: 4 (over z), col: 8 (over y, x, core).
Axes of the slice: x: 2, y: 2, z: 4, core: 2. Of those that a mesh axis runs over, the one named last changes fastest.
Arguments:
- right_side: float32 [4096, 4, 128], P(('row', 'col')), may hold values from -60 to 60
- cluster_of: int32 [4096], P(('row', 'col')), may hold values from 0 to 4095, as said below
- near_rows: int32 [12288], P(('row', 'col')), may hold values from 0 to 127
- near_columns: int32 [12288], P(('row', 'col')), may hold values from 0 to 191, as said below
- near_blocks: bfloat16 [12288, 128, 128], P(('row', 'col')), may hold values from -1 to 1
- far_rows: int32 [32768], P(('row', 'col')), may hold values from 0 to 1023, as said below
- far_columns: int32 [32768], P(('row', 'col')), may hold values from 0 to 511
- far_rank: int32 [32768], P(('row', 'col')), may hold values from 4 to 16
- far_left: bfloat16 [32768, 16, 128], P(('row', 'col')), may hold values from -1.5 to 1.5
- far_right: bfloat16 [32768, 16, 128], P(('row', 'col')), may hold values from -0.5 to 0.5
Outputs:
- second_basis: float32 [4096, 4, 128], P(('row', 'col'))
- next_vector: float32 [4096, 4, 128], P(('row', 'col'))
- hessenberg: float32 [5, 4], replicated
Inputs may be any that keep to these rules, and one draw needn't show every extreme that they name: `cluster_of`: A permutation of the cluster positions; position g belongs to the device of index g // 128 along row+col. Each device's blocks go to at most 8 blocks a destination device, and exactly 8 to some. `near_columns`: position 32 is the device's own first block; entries never point before the first or after the last block of cluster order. `far_rows`: in each device's list, the k-th group of 128 entries has rows in blocks k * 128 to (k + 1) * 128 - 1 of the row cluster.
All inputs are finite; a program needn't handle non-finite values.
Results may differ from a plain program's by a relative error of at most 0.0018.
The roundings to bfloat16 on the way count: a program that leaves them out, or rounds other values in their place, can miss the bound.
Values may be sent and summed in bfloat16 or wider, within the bound.
A program may use at most 128 MiB of HBM per device.

v0:
```python
import jax
import jax.numpy as jnp
from jax import lax
from jax.sharding import PartitionSpec as P

epsilon = 1e-06


def padded(cells, sides, width):
    for axis, dim in sides:
        count = lax.axis_size(axis)
        ends = count - 1
        head = lax.slice_in_dim(cells, 0, width, axis=dim)
        tail = lax.slice_in_dim(cells, cells.shape[dim] - width, cells.shape[dim], axis=dim)
        cells = jnp.concatenate(
            [
                lax.ppermute(tail, axis, [(i, (i + 1) % count) for i in range(ends)]),
                cells,
                lax.ppermute(head, axis, [((i + 1) % count, i) for i in range(ends)]),
            ],
            axis=dim,
        )
    return cells


def body(
    right_side,
    cluster_of,
    near_rows,
    near_columns,
    near_blocks,
    far_rows,
    far_columns,
    far_rank,
    far_left,
    far_right,
):
    row_count = lax.axis_size("row")
    column_count = lax.axis_size("col")
    device_count = row_count * column_count
    local_blocks = right_side.shape[0]
    sides = right_side.shape[1]
    width = right_side.shape[2]
    capacity = 2 * local_blocks // device_count
    halo_width = local_blocks // 4
    panels = local_blocks * device_count * width
    max_rank = far_left.shape[1]
    target = cluster_of // local_blocks
    place = cluster_of % local_blocks
    order = jnp.arange(local_blocks, dtype=jnp.int32)
    earlier = (target[None, :] == target[:, None]) & (order[None, :] < order[:, None])
    slot_index = jnp.sum(earlier.astype(jnp.int32), axis=1)
    position_send = (
        jnp.full((device_count, capacity), local_blocks, jnp.int32)
        .at[target, slot_index]
        .set(place)
    )
    position_recv = lax.all_to_all(
        position_send, ("row", "col"), split_axis=0, concat_axis=0, tiled=True
    ).reshape(-1)
    fetch_index = jnp.minimum(position_recv, local_blocks - 1)
    rank_mask = (jnp.arange(max_rank, dtype=jnp.int32)[None, :] < far_rank[:, None]).astype(
        jnp.float32
    )[:, :, None]

    def relay_in(vector):
        rounded = vector.astype(jnp.bfloat16)
        outgoing = (
            jnp.zeros((device_count, capacity, sides, width), jnp.bfloat16)
            .at[target, slot_index]
            .set(rounded)
        )
        arrived = lax.all_to_all(outgoing, ("row", "col"), split_axis=0, concat_axis=0, tiled=True)
        arrived = arrived.reshape(device_count * capacity, sides, width)
        return (
            jnp.zeros((local_blocks, sides, width), jnp.bfloat16)
            .at[position_recv]
            .set(arrived, mode="drop")
        )

    def relay_out(image_sum):
        outgoing = image_sum[fetch_index].reshape(device_count, capacity, sides, width)
        returned = lax.all_to_all(outgoing, ("row", "col"), split_axis=0, concat_axis=0, tiled=True)
        return returned[target, slot_index]

    def apply_clustered(clustered):
        extended = padded(clustered, ((("row", "col"), 0),), halo_width)
        near_out = jnp.einsum(
            "ekp,eqp->eqk", near_blocks, extended[near_columns], preferred_element_type=jnp.float32
        )
        image_sum = 0.5 * clustered.astype(jnp.float32)
        image_sum = image_sum.at[near_rows].add(near_out)
        gathered = lax.all_gather(clustered, "row", axis=0, tiled=True)
        coefficients = jnp.einsum(
            "etp,eqp->etq", far_right, gathered[far_columns], preferred_element_type=jnp.float32
        )
        coefficients = (coefficients * rank_mask).astype(jnp.bfloat16)
        far_out = jnp.einsum(
            "etq,etk->eqk", coefficients, far_left, preferred_element_type=jnp.float32
        )
        partial_value = (
            jnp.zeros((local_blocks * column_count, sides, width), jnp.float32)
            .at[far_rows]
            .add(far_out)
        )
        image_sum = image_sum + lax.psum_scatter(
            partial_value, "col", scatter_dimension=0, tiled=True
        )
        return image_sum

    def operate_mesh(vector):
        return relay_out(apply_clustered(relay_in(vector)))

    def local_inner(left_vector, right_vector):
        return jnp.sum(left_vector * right_vector, axis=(0, 2))

    side_norm = jnp.sqrt(
        lax.psum(local_inner(right_side, right_side), ("row", "col")) / panels + epsilon
    )
    first = right_side / side_norm[None, :, None]
    image_one = operate_mesh(first)
    project_one = lax.psum(local_inner(first, image_one), ("row", "col")) / panels
    remainder = image_one - project_one[None, :, None] * first
    norm_two = jnp.sqrt(
        lax.psum(local_inner(remainder, remainder), ("row", "col")) / panels + epsilon
    )
    second_basis = remainder / norm_two[None, :, None]
    image_two = operate_mesh(second_basis)
    sum_two, sum_three = lax.psum(
        (local_inner(first, image_two), local_inner(second_basis, image_two)), ("row", "col")
    )
    project_two = sum_two / panels
    project_three = sum_three / panels
    next_vector = (
        image_two - project_two[None, :, None] * first - project_three[None, :, None] * second_basis
    )
    second_basis, next_vector, entries = (
        second_basis,
        next_vector,
        (project_one, norm_two, project_two, project_three),
    )
    project_one, norm_two, project_two, project_three = entries
    hessenberg = jnp.stack([side_norm, project_one, norm_two, project_two, project_three])
    return (second_basis, next_vector, hessenberg)


def solution(mesh):
    placed = (
        P(("row", "col"), None, None),
        P(("row", "col")),
        P(("row", "col")),
        P(("row", "col")),
        P(("row", "col"), None, None),
        P(("row", "col")),
        P(("row", "col")),
        P(("row", "col")),
        P(("row", "col"), None, None),
        P(("row", "col"), None, None),
    )
    return jax.shard_map(
        body,
        mesh=mesh,
        in_specs=placed,
        out_specs=(P(("row", "col"), None, None), P(("row", "col"), None, None), P()),
        check_vma=False,
    )
```

profile of v0, /device:TPU:0, one launch (start us, length us, event | category | flops | bytes accessed | tf_op | source)
XLA Modules:
  0.0 641.9 jit_solution(10303565593195334214)
XLA Ops:
  7.2 0.7 and_select_fusion
  7.9 0.2 convert_reduce_fusion
  8.1 6.4 %scatter_fusion = s32[32,8]{0,1:T(8,128)S(1)} fusion(s32[32,8]{0,1:T(8,128)S(1)} %broadcast_in_dim.12, s32[128]{0:T(128)S(1)} %get-tuple-element.28, s32[128]{0:T(128)S(1)} %get-tuple-element.41), kind=kCustom, calls=%fused_computation.8 | custom fusion | bytes 2560 | tf_op jit(solution)/shard_map/scatter | solution.py:56
  14.5 0.7 copy.18
  15.2 7.3 %all-to-all-start = ((s32[32,1,8]{2,1,0:T(1,128)}), s32[32,1,8]{2,1,0:T(1,128)S(1)}, u32[]{:S(2)}, u32[]{:S(2)}) async-start(s32[32,1,8]{2,1,0:T(1,128)} %copy.18), calls=%async_computation | async-start | bytes 32768 | tf_op jit(solution)/shard_map/all_to_all | solution.py:58
  22.5 1.2 multiply_reduce_fusion.4
  23.7 0.7 compare_select_fusion.1
  24.4 40.5 %psum.35 = f32[4]{0:T(128)S(1)} all-reduce(f32[4]{0:T(128)S(1)} %multiply_reduce_fusion.4), channel_id=1, replica_groups=mesh['row'=4,'col'=8] {'row','col'}, use_global_device_ids=true, to_apply=%region_3.4 | all-reduce | flops 4 | bytes 32 | tf_op jit(solution)/shard_map/psum | solution.py:118
  64.9 1.1 fusion.17
  66.1 0.8 broadcast.143.clone
  66.8 14.8 %scatter_fusion.1 = bf16[32,8,4,128]{3,2,1,0:T(4,128)(2,1)} fusion(bf16[32,8,4,128]{3,2,1,0:T(4,128)(2,1)} %broadcast.143.clone, s32[128]{0:T(128)S(1)} %get-tuple-element.28, bf16[128,4,128]{2,1,0:T(4,128)(2,1)S(1)} %get-tuple-element.21), kind=kCustom, calls=%fused_computation.9 | custom fusion | bytes 394240 | tf_op jit(solution)/shard_map/scatter | solution.py:71
  81.6 4.5 all-to-all-start.1
  86.2 0.6 dynamic-slice
  87.4 0.2 fusion.4
  87.6 0.5 broadcast.352
  88.1 0.7 reduce.3
  88.9 7.8 %all-to-all-done.1 = bf16[32,8,4,128]{3,2,1,0:T(4,128)(2,1)S(1)} async-done(((bf16[32,8,4,128]{3,2,1,0:T(4,128)(2,1)}), bf16[32,8,4,128]{3,2,1,0:T(4,128)(2,1)S(1)}, u32[]{:S(2)}, u32[]{:S(2)}) %all-to-all-start.1) | async-done | bytes 262176 | tf_op jit(solution)/shard_map/all_to_all | solution.py:73
  96.7 7.3 %scatter_fusion.2 = bf16[128,4,128]{2,1,0:T(4,128)(2,1)S(1)} fusion(bf16[128,4,128]{2,1,0:T(4,128)(2,1)S(1)} %broadcast.137.clone, s32[256]{0:T(256)S(1)} %bitcast.57, bf16[256,4,128]{2,1,0:T(4,128)(2,1)S(1)} %bitcast.55), kind=kCustom, calls=%fused_computation.10 | custom fusion | bytes 787456 | tf_op jit(solution)/shard_map/scatter | solution.py:78
  104.1 15.9 %all_gather.6 = bf16[512,4,128]{2,1,0:T(4,128)(2,1)S(1)} all-gather(bf16[128,4,128]{2,1,0:T(4,128)(2,1)S(1)} %scatter_fusion.2), channel_id=1, replica_groups=mesh['row'=4,'col'=8] {'row'}, dimensions={0}, use_global_device_ids=true | all-gather | bytes 655360 | tf_op jit(solution)/shard_map/all_gather | solution.py:93
  120.0 3.6 gather_fusion
  123.5 8.3 %fusion = f32[1024,4,128]{2,1,0:T(4,128)} fusion(bf16[1024,16,128]{2,1,0:T(8,128)(2,1)} %param.18, bf16[1024,4,128]{2,1,0:T(4,128)(2,1)S(1)} %gather_fusion, bf16[1024,16,128]{2,1,0:T(8,128)(2,1)} %param.19, f32[1024,16]{1,0:T(8,128)S(1)} %fusion.4), kind=kOutput, calls=%fused_computation.19 | convolution fusion | flops 33685504 | bytes 11599872 | tf_op jit(solution)/shard_map/etq,etk->eqk/dot_general | solution.py:98
  131.8 0.3 broadcast.147.clone
  132.1 66.4 %scatter_fusion.3 = f32[1024,4,128]{2,1,0:T(4,128)S(1)} fusion(f32[1024,4,128]{2,1,0:T(4,128)S(1)} %broadcast.147.clone, s32[1024]{0:T(1024)S(1)} %compare_select_fusion.1, f32[1024,4,128]{2,1,0:T(4,128)} %fusion), kind=kCustom, calls=%fused_computation.11 | custom fusion | flops 524288 | bytes 6295552 | tf_op jit(solution)/shard_map/scatter-add | solution.py:104
  198.5 1.3 copy-done.1
  199.9 1.3 collective-permute-start.1
  201.2 3.0 collective-permute-start
  204.3 0.8 collective-permute-done
  205.2 2.0 gather_fusion.1
  207.3 9.6 %fusion.20 = f32[384,4,128]{2,1,0:T(4,128)S(1)} fusion(bf16[384,4,128]{2,1,0:T(4,128)(2,1)S(1)} %gather_fusion.1, bf16[384,128,128]{2,1,0:T(8,128)(2,1)} %param.14), kind=kOutput, calls=%fused_computation.78 | convolution fusion | flops 50331648 | bytes 13762560 | tf_op jit(solution)/shard_map/ekp,eqp->eqk/dot_general | solution.py:88
  216.9 42.1 %all-reduce.6.cloned.1.call-done = f32[1024,4,128]{2,1,0:T(4,128)} async-done(((f32[1024,4,128]{2,1,0:T(4,128)}), f32[1024,4,128]{2,1,0:T(4,128)}) %all-reduce.6.cloned.1.call-update) | async-done | bytes 2097168
  258.9 1.0 dynamic-slice_add_fusion.1
  260.0 14.3 %scatter_fusion.4 = f32[128,4,128]{2,1,0:T(4,128)S(1)} fusion(f32[128,4,128]{2,1,0:T(4,128)S(1)} %dynamic-slice_add_fusion.1, s32[384]{0:T(512)S(1)} %compare_select_fusion.5, f32[384,4,128]{2,1,0:T(4,128)S(1)} %fusion.20), kind=kCustom, calls=%fused_computation.12 | custom fusion | flops 196608 | bytes 2360832 | tf_op jit(solution)/shard_map/scatter-add | solution.py:92
  274.2 1.0 gather_fusion.2
  275.2 19.2 %all_to_all.29 = f32[32,8,4,128]{3,2,1,0:T(4,128)S(1)} all-to-all(f32[32,8,4,128]{3,2,1,0:T(4,128)S(1)} %bitcast.54), channel_id=1, replica_groups=mesh['row'=4,'col'=8] {'row','col'}, dimensions={0} | all-to-all | bytes 1048576 | tf_op jit(solution)/shard_map/all_to_all | solution.py:83
  294.4 0.9 gather_fusion.3
  295.3 0.3 multiply_reduce_fusion.3
  295.6 39.0 %psum.36 = f32[4]{0:T(128)S(1)} all-reduce(f32[4]{0:T(128)S(1)} %multiply_reduce_fusion.3), channel_id=1, replica_groups=mesh['row'=4,'col'=8] {'row','col'}, use_global_device_ids=true, to_apply=%region_10.11 | all-reduce | flops 4 | bytes 32 | tf_op jit(solution)/shard_map/psum | solution.py:122
  334.6 0.3 multiply_reduce_fusion.2
  334.9 40.0 %psum.37 = f32[4]{0:T(128)S(1)} all-reduce(f32[4]{0:T(128)S(1)} %multiply_reduce_fusion.2), channel_id=1, replica_groups=mesh['row'=4,'col'=8] {'row','col'}, use_global_device_ids=true, to_apply=%region_12.13 | all-reduce | flops 4 | bytes 32 | tf_op jit(solution)/shard_map/psum | solution.py:125
  374.9 0.2 fusion.16
  375.2 5.7 scatter_fusion.5
  380.9 14.6 %all_to_all.30 = bf16[32,8,4,128]{3,2,1,0:T(4,128)(2,1)S(1)} all-to-all(bf16[32,8,4,128]{3,2,1,0:T(4,128)(2,1)S(1)} %scatter_fusion.5), channel_id=1, replica_groups=mesh['row'=4,'col'=8] {'row','col'}, dimensions={0} | all-to-all | bytes 524288 | tf_op jit(solution)/shard_map/all_to_all | solution.py:73
  395.6 7.3 %scatter_fusion.6 = bf16[128,4,128]{2,1,0:T(4,128)(2,1)S(1)} fusion(bf16[128,4,128]{2,1,0:T(4,128)(2,1)S(1)} %broadcast.137, s32[256]{0:T(256)S(1)} %bitcast.58, bf16[256,4,128]{2,1,0:T(4,128)(2,1)S(1)} %bitcast.56), kind=kCustom, calls=%fused_computation.14 | custom fusion | bytes 787456 | tf_op jit(solution)/shard_map/scatter | solution.py:78
  402.9 15.9 %all_gather.7 = bf16[512,4,128]{2,1,0:T(4,128)(2,1)S(1)} all-gather(bf16[128,4,128]{2,1,0:T(4,128)(2,1)S(1)} %scatter_fusion.6), channel_id=1, replica_groups=mesh['row'=4,'col'=8] {'row'}, dimensions={0}, use_global_device_ids=true | all-gather | bytes 655360 | tf_op jit(solution)/shard_map/all_gather | solution.py:93
  418.8 3.6 gather_fusion.4
  422.4 8.3 %fusion.1 = f32[1024,4,128]{2,1,0:T(4,128)} fusion(bf16[1024,16,128]{2,1,0:T(8,128)(2,1)} %param.18, bf16[1024,4,128]{2,1,0:T(4,128)(2,1)S(1)} %gather_fusion.4, bf16[1024,16,128]{2,1,0:T(8,128)(2,1)} %param.19, f32[1024,16]{1,0:T(8,128)S(1)} %fusion.4), kind=kOutput, calls=%fused_computation.20 | convolution fusion | flops 33685504 | bytes 11599872 | tf_op jit(solution)/shard_map/etq,etk->eqk/dot_general | solution.py:98
  430.7 0.3 broadcast.147
  431.0 66.4 %scatter_fusion.7 = f32[1024,4,128]{2,1,0:T(4,128)S(1)} fusion(f32[1024,4,128]{2,1,0:T(4,128)S(1)} %broadcast.147, s32[1024]{0:T(1024)S(1)} %compare_select_fusion.1, f32[1024,4,128]{2,1,0:T(4,128)} %fusion.1), kind=kCustom, calls=%fused_computation.15 | custom fusion | flops 524288 | bytes 6295552 | tf_op jit(solution)/shard_map/scatter-add | solution.py:104
  497.4 1.3 copy-done
  498.7 1.3 collective-permute-start.3
  500.0 3.0 collective-permute-start.2
  503.1 0.8 collective-permute-done.2
  504.0 2.0 gather_fusion.5
  506.1 9.6 %fusion.21 = f32[384,4,128]{2,1,0:T(4,128)S(1)} fusion(bf16[384,4,128]{2,1,0:T(4,128)(2,1)S(1)} %gather_fusion.5, bf16[384,128,128]{2,1,0:T(8,128)(2,1)} %param.14), kind=kOutput, calls=%fused_computation.79 | convolution fusion | flops 50331648 | bytes 13762560 | tf_op jit(solution)/shard_map/ekp,eqp->eqk/dot_general | solution.py:88
  515.7 42.1 %all-reduce.8.cloned.1.call-done = f32[1024,4,128]{2,1,0:T(4,128)} async-done(((f32[1024,4,128]{2,1,0:T(4,128)}), f32[1024,4,128]{2,1,0:T(4,128)}) %all-reduce.8.cloned.1.call-update) | async-done | bytes 2097168
  557.8 1.0 dynamic-slice_add_fusion
  558.8 14.3 %scatter_fusion.8 = f32[128,4,128]{2,1,0:T(4,128)S(1)} fusion(f32[128,4,128]{2,1,0:T(4,128)S(1)} %dynamic-slice_add_fusion, s32[384]{0:T(512)S(1)} %compare_select_fusion.5, f32[384,4,128]{2,1,0:T(4,128)S(1)} %fusion.21), kind=kCustom, calls=%fused_computation.16 | custom fusion | flops 196608 | bytes 2360832 | tf_op jit(solution)/shard_map/scatter-add | solution.py:92
  573.1 1.0 gather_fusion.6
  574.1 19.2 %all_to_all.31 = f32[32,8,4,128]{3,2,1,0:T(4,128)S(1)} all-to-all(f32[32,8,4,128]{3,2,1,0:T(4,128)S(1)} %bitcast.53), channel_id=1, replica_groups=mesh['row'=4,'col'=8] {'row','col'}, dimensions={0} | all-to-all | bytes 1048576 | tf_op jit(solution)/shard_map/all_to_all | solution.py:83
  593.3 0.9 gather_fusion.7
  594.2 0.3 multiply_reduce_fusion.1
  594.5 39.0 %all-reduce.2 = (f32[4]{0:T(128)S(1)}, f32[4]{0:T(128)S(1)}) all-reduce(f32[4]{0:T(128)S(1)} %get-tuple-element.16, f32[4]{0:T(128)S(1)} %get-tuple-element.15), channel_id=1, replica_groups=mesh['row'=4,'col'=8] {'row','col'}, use_global_device_ids=true, to_apply=%region_21.22 | all-reduce | flops 8 | bytes 64 | tf_op jit(solution)/shard_map/psum | solution.py:129
  633.5 0.7 copy.19
  634.2 0.9 multiply_subtract_fusion
  (42 shorter events, 0.8 us)
Async XLA Ops:
  7.2 79.0 %copy-start.7 = (u32[32]{0:T(128)S(1)}, u32[32]{0:T(128)}, u32[]{:S(2)}) copy-start(u32[32]{0:T(128)} %constant.140) | copy-start | bytes 388
  7.2 58.8 %copy-start.4 = (s32[1024]{0:T(1024)S(1)}, s32[1024]{0:T(1024)}, u32[]{:S(2)}) copy-start(s32[1024]{0:T(1024)} %param.16) | copy-start | bytes 12292
  7.2 58.8 %copy-start.5 = (s32[384]{0:T(512)S(1)}, s32[384]{0:T(512)}, u32[]{:S(2)}) copy-start(s32[384]{0:T(512)} %param.12) | copy-start | bytes 4612
  7.2 58.8 %copy-start.6 = (s32[384]{0:T(512)S(1)}, s32[384]{0:T(512)}, u32[]{:S(2)}) copy-start(s32[384]{0:T(512)} %param.13) | copy-start | bytes 4612
  7.2 80.2 %copy-start.3 = (s32[1024]{0:T(1024)S(1)}, s32[1024]{0:T(1024)}, u32[]{:S(2)}) copy-start(s32[1024]{0:T(1024)} %param.17) | copy-start | bytes 12292
  15.2 66.4 %all-to-all-start = ((s32[32,1,8]{2,1,0:T(1,128)}), s32[32,1,8]{2,1,0:T(1,128)S(1)}, u32[]{:S(2)}, u32[]{:S(2)}) async-start(s32[32,1,8]{2,1,0:T(1,128)} %copy.18), calls=%async_computation | async-start | bytes 32768 | tf_op jit(solution)/shard_map/all_to_all | solution.py:58
  81.6 15.1 %all-to-all-start.1 = ((bf16[32,8,4,128]{3,2,1,0:T(4,128)(2,1)}), bf16[32,8,4,128]{3,2,1,0:T(4,128)(2,1)S(1)}, u32[]{:S(2)}, u32[]{:S(2)}) async-start(bf16[32,8,4,128]{3,2,1,0:T(4,128)(2,1)} %scatter_fusion.1), calls=%async_computation.1 | async-start | bytes 524288 | tf_op jit(solution)/shard_map/all_to_all | solution.py:73
  86.1 172.8 %all-reduce.6.cloned.1.call-start = ((), (), s32[]{:S(2)}) async-start(), calls=%async_computation.5 | async-start | bytes 4194304
  198.5 1.3 copy-start.1
  199.8 358.0 %all-reduce.8.cloned.1.call-start = ((), (), s32[]{:S(2)}) async-start(), calls=%async_computation.6 | async-start | bytes 4194304
  199.9 4.4 collective-permute-start.1
  201.2 3.9 collective-permute-start
  375.1 259.1 %copy-start.2 = (f32[128,4,128]{2,1,0:T(4,128)}, f32[128,4,128]{2,1,0:T(4,128)S(1)}, u32[]{:S(2)}) copy-start(f32[128,4,128]{2,1,0:T(4,128)S(1)} %get-tuple-element.20) | copy-start | bytes 786436
  497.4 1.3 copy-start
  498.7 4.3 collective-permute-start.3
  500.0 3.9 collective-permute-start.2
Sparse Core Ops, SparseCore 0:
  199.9 58.9 all-reduce.5
  498.8 58.9 all-reduce.7
where the time goes:
time: 652 us; the launch traced here: 642 us
  blocking collectives  243 us (37%)
  other arithmetic  170 us (26%)
  waiting for transfers between devices  93.6 us (14%)
  local copies, waits for them, and re-layouts  63.2 us (10%)
  matrix products  35.8 us (5%)
  starting transfers between devices  20.5 us (3%)
  between operations  15.1 us (2%)
    scatter-add x2, other arithmetic, apply_clustered(): partial_value = jnp.zeros((local_blocks * column_count, sides, width), jn...  133 us
    unnamed x4, waiting for transfers between devices  84.2 us
    psum x1, blocking collectives, body(): lax.psum(local_inner(right_side, right_side), ('row', 'col')) / panels  40.5 us
    psum x1, blocking collectives, body(): lax.psum(local_inner(remainder, remainder), ('row', 'col')) / panels  40 us
    psum x1, blocking collectives, body(): lax.psum((local_inner(first, image_two), local_inner(second_basis, image_...  39 us
    psum x1, blocking collectives, body(): lax.psum(local_inner(first, image_one), ('row', 'col')) / panels  39 us
    all_to_all x2, blocking collectives, relay_out(): lax.all_to_all(outgoing, ('row', 'col'), split_axis=0, concat_axis=0, til...  38.3 us
    all_gather x2, blocking collectives, apply_clustered(): gathered = lax.all_gather(clustered, 'row', axis=0, tiled=True)  31.8 us
  transfers between devices with their start and end apart: 8, of which 5 were waited for; matrix products, arithmetic and copies ran while one was open for 7% of the time, Pallas kernels for 0%

commit v1 on v0

v1 whole, which is shorter than its diff:
```python
import functools

import jax
import jax.numpy as jnp
from jax import lax
from jax.experimental import pallas as pl
from jax.experimental.pallas import tpu as pltpu
from jax.sharding import PartitionSpec as P

epsilon = 1e-06
MESH = pl.DeviceIdType.MESH
HIGH = lax.Precision.HIGHEST
VMEM = pl.BlockSpec(memory_space=pltpu.VMEM)
LANES = 128
LIMIT = 56 * 2**20


def coordinates(index, column_count):
    return (lax.div(index, column_count), lax.rem(index, column_count))


def enter(me, rows, columns):
    count = rows * columns
    barrier = pltpu.get_barrier_semaphore()

    @pl.loop(1, count)
    def _(k):
        pl.semaphore_signal(
            barrier,
            inc=1,
            device_id=coordinates(lax.rem(me + k, count), columns),
            device_id_type=MESH,
        )

    pl.semaphore_wait(barrier, count - 1)


def exchange_kernel(rows, columns, send_ref, recv_ref, send_sem, recv_sem):
    count = rows * columns
    me = lax.axis_index("row") * columns + lax.axis_index("col")
    enter(me, rows, columns)

    def copy(k):
        peer = lax.rem(me + k, count)
        return pltpu.make_async_remote_copy(
            src_ref=send_ref.at[peer],
            dst_ref=recv_ref.at[me],
            send_sem=send_sem.at[k],
            recv_sem=recv_sem.at[k],
            device_id=coordinates(peer, columns),
            device_id_type=MESH,
        )

    def arrival(k):
        source = lax.rem(me + count - k, count)
        return pltpu.make_async_remote_copy(
            src_ref=send_ref.at[source],
            dst_ref=recv_ref.at[source],
            send_sem=send_sem.at[k],
            recv_sem=recv_sem.at[k],
            device_id=coordinates(source, columns),
            device_id_type=MESH,
        )

    @pl.loop(1, count)
    def _(k):
        copy(k).start()

    recv_ref[me] = send_ref[me]

    @pl.loop(1, count)
    def _(k):
        arrival(k).wait_recv()

    @pl.loop(1, count)
    def _(k):
        copy(k).wait_send()


def exchange(send, rows, columns, collective_id):
    count = rows * columns
    return pl.pallas_call(
        functools.partial(exchange_kernel, rows, columns),
        out_shape=jax.ShapeDtypeStruct(send.shape, send.dtype),
        in_specs=[VMEM],
        out_specs=VMEM,
        scratch_shapes=[
            pltpu.SemaphoreType.DMA((count,)),
            pltpu.SemaphoreType.DMA((count,)),
        ],
        compiler_params=pltpu.CompilerParams(
            collective_id=collective_id, has_side_effects=True, vmem_limit_bytes=LIMIT
        ),
    )(send)


def spread_densities(rows, columns, own_ref, all_ref, left_ref, right_ref, send_sem, recv_sem):
    row, column = lax.axis_index("row"), lax.axis_index("col")
    count = rows * columns
    me = row * columns + column
    halo = left_ref.shape[0]
    blocks = own_ref.shape[0]
    after = coordinates(lax.rem(me + 1, count), columns)
    before = coordinates(lax.rem(me + count - 1, count), columns)
    halos = [
        pltpu.make_async_remote_copy(
            src_ref=own_ref.at[pl.ds(blocks - halo, halo)],
            dst_ref=left_ref,
            send_sem=send_sem.at[0],
            recv_sem=recv_sem.at[0],
            device_id=after,
            device_id_type=MESH,
        ),
        pltpu.make_async_remote_copy(
            src_ref=own_ref.at[pl.ds(0, halo)],
            dst_ref=right_ref,
            send_sem=send_sem.at[rows],
            recv_sem=recv_sem.at[rows],
            device_id=before,
            device_id_type=MESH,
        ),
    ]
    for copy in halos:
        copy.start()
    copies = []
    for k in range(1, rows):
        copies.append(
            pltpu.make_async_remote_copy(
                src_ref=own_ref,
                dst_ref=all_ref.at[row],
                send_sem=send_sem.at[k],
                recv_sem=recv_sem.at[k],
                device_id=(lax.rem(row + k, rows), column),
                device_id_type=MESH,
            )
        )
        copies[-1].start()
    all_ref[row] = own_ref[...]
    for copy in halos:
        copy.wait()
    for k in range(1, rows):
        source = lax.rem(row + rows - k, rows)
        pltpu.make_async_remote_copy(
            src_ref=own_ref,
            dst_ref=all_ref.at[source],
            send_sem=send_sem.at[k],
            recv_sem=recv_sem.at[k],
            device_id=(source, column),
            device_id_type=MESH,
        ).wait_recv()
    for copy in copies:
        copy.wait_send()


def spread_kernel(rows, columns, own_ref, all_ref, left_ref, right_ref, send_sem, recv_sem):
    enter(lax.axis_index("row") * columns + lax.axis_index("col"), rows, columns)
    spread_densities(rows, columns, own_ref, all_ref, left_ref, right_ref, send_sem, recv_sem)


def density_shapes(blocks, width, rows):
    halo = blocks // 4
    return [
        jax.ShapeDtypeStruct((rows, blocks, width), jnp.bfloat16),
        jax.ShapeDtypeStruct((halo, width), jnp.bfloat16),
        jax.ShapeDtypeStruct((halo, width), jnp.bfloat16),
    ]


def spread(own, rows, columns, collective_id):
    return pl.pallas_call(
        functools.partial(spread_kernel, rows, columns),
        out_shape=density_shapes(own.shape[0], own.shape[1], rows),
        in_specs=[VMEM],
        out_specs=[VMEM] * 3,
        scratch_shapes=[
            pltpu.SemaphoreType.DMA((rows + 1,)),
            pltpu.SemaphoreType.DMA((rows + 1,)),
        ],
        compiler_params=pltpu.CompilerParams(
            collective_id=collective_id, has_side_effects=True, vmem_limit_bytes=LIMIT
        ),
    )(own)


def split_dot(picker, value):
    high = value.astype(jnp.bfloat16)
    rest = value - high.astype(jnp.float32)
    middle = rest.astype(jnp.bfloat16)
    low = (rest - middle.astype(jnp.float32)).astype(jnp.bfloat16)
    dot = functools.partial(jnp.dot, picker, preferred_element_type=jnp.float32)
    return dot(high) + (dot(middle) + dot(low))


def one_hot(condition):
    return jnp.where(condition, 1.0, 0.0).astype(jnp.bfloat16)


def operator_kernel(
    sides,
    own_ref,
    all_ref,
    left_ref,
    right_ref,
    near_column_ref,
    near_row_ref,
    far_column_ref,
    far_row_ref,
    owner_ref,
    near_ref,
    far_left_ref,
    far_right_ref,
    image_ref,
    partial_ref,
    extended,
    near_picked,
    near_out,
    far_picked,
    far_out,
):
    step = pl.program_id(0)
    blocks = own_ref.shape[0]
    halo = left_ref.shape[0]
    rows = all_ref.shape[0]
    near_count = near_ref.shape[0]
    far_count = far_left_ref.shape[0]
    rank = far_left_ref.shape[1]
    width = sides * LANES
    nt = (((1,), (1,)), ((), ()))

    @pl.when(step == 0)
    def _():
        extended[0:halo] = left_ref[...]
        extended[halo : halo + blocks] = own_ref[...]
        extended[halo + blocks :] = right_ref[...]
        image_ref[...] = 0.5 * own_ref[...].astype(jnp.float32)

    reach = blocks + 2 * halo
    pick = one_hot(
        near_column_ref[...] == lax.broadcasted_iota(jnp.int32, (near_count, reach), 1)
    )
    near_picked[...] = jnp.dot(pick, extended[...], preferred_element_type=jnp.float32)
    batch = 8
    row_id = lax.rem(lax.broadcasted_iota(jnp.int32, (sides * batch, LANES), 0), batch)
    for j in range(near_count // batch):
        here = slice(j * batch, (j + 1) * batch)
        stacked = jnp.concatenate(
            [near_picked[here, s * LANES : (s + 1) * LANES] for s in range(sides)], axis=0
        ).astype(jnp.bfloat16)
        product = lax.dot_general(
            stacked,
            near_ref[here].reshape(batch * LANES, LANES),
            nt,
            preferred_element_type=jnp.float32,
        )
        value = jnp.zeros((sides * batch, LANES), jnp.float32)
        for e in range(batch):
            value = jnp.where(row_id == e, product[:, e * LANES : (e + 1) * LANES], value)
        for s in range(sides):
            near_out[here, s * LANES : (s + 1) * LANES] = value[s * batch : (s + 1) * batch]
    place = one_hot(
        near_row_ref[0] == lax.broadcasted_iota(jnp.int32, (blocks, near_count), 0)
    )
    image_ref[...] += split_dot(place, near_out[...])

    pick = one_hot(
        far_column_ref[...] == lax.broadcasted_iota(jnp.int32, (far_count, rows * blocks), 1)
    )
    far_picked[...] = jnp.dot(
        pick, all_ref[...].reshape(rows * blocks, width), preferred_element_type=jnp.float32
    )
    batch = 32
    row_id = lax.rem(lax.broadcasted_iota(jnp.int32, (sides * batch, batch * rank), 0), batch)
    for j in range(far_count // batch):
        here = slice(j * batch, (j + 1) * batch)
        stacked = jnp.concatenate(
            [far_picked[here, s * LANES : (s + 1) * LANES] for s in range(sides)], axis=0
        ).astype(jnp.bfloat16)
        product = lax.dot_general(
            stacked,
            far_right_ref[here].reshape(batch * rank, LANES),
            nt,
            preferred_element_type=jnp.float32,
        )
        coefficients = jnp.where(row_id == owner_ref[0, j : j + 1], product, 0.0).astype(
            jnp.bfloat16
        )
        value = jnp.dot(
            coefficients,
            far_left_ref[here].reshape(batch * rank, LANES),
            preferred_element_type=jnp.float32,
        )
        for s in range(sides):
            far_out[here, s * LANES : (s + 1) * LANES] = value[s * batch : (s + 1) * batch]
    place = one_hot(far_row_ref[0] == lax.broadcasted_iota(jnp.int32, (blocks, far_count), 0))
    partial_ref[0] = split_dot(place, far_out[...])


def operate(densities, own, tables, near_blocks, far_left, far_right, sides, groups):
    everything, left, right = densities
    near_column, near_row, far_column, far_row, owner = tables
    blocks, width = own.shape
    near_count = near_blocks.shape[0] // groups
    far_count = far_left.shape[0] // groups
    rank = far_left.shape[1]
    chunks = owner.shape[1]
    return pl.pallas_call(
        functools.partial(operator_kernel, sides),
        grid=(groups,),
        out_shape=[
            jax.ShapeDtypeStruct((blocks, width), jnp.float32),
            jax.ShapeDtypeStruct((groups, blocks, width), jnp.float32),
        ],
        in_specs=[
            VMEM,
            VMEM,
            VMEM,
            VMEM,
            pl.BlockSpec((near_count, 1), lambda i: (i, 0)),
            pl.BlockSpec((1, 1, near_count), lambda i: (i, 0, 0)),
            pl.BlockSpec((far_count, 1), lambda i: (i, 0)),
            pl.BlockSpec((1, 1, far_count), lambda i: (i, 0, 0)),
            pl.BlockSpec((1, chunks, owner.shape[2]), lambda i: (i, 0, 0)),
            pl.BlockSpec((near_count, LANES, LANES), lambda i: (i, 0, 0)),
            pl.BlockSpec((far_count, rank, LANES), lambda i: (i, 0, 0)),
            pl.BlockSpec((far_count, rank, LANES), lambda i: (i, 0, 0)),
        ],
        out_specs=[
            pl.BlockSpec((blocks, width), lambda i: (0, 0)),
            pl.BlockSpec((1, blocks, width), lambda i: (i, 0, 0)),
        ],
        scratch_shapes=[
            pltpu.VMEM((blocks + 2 * left.shape[0], width), jnp.bfloat16),
            pltpu.VMEM((near_count, width), jnp.float32),
            pltpu.VMEM((near_count, width), jnp.float32),
            pltpu.VMEM((far_count, width), jnp.float32),
            pltpu.VMEM((far_count, width), jnp.float32),
        ],
        compiler_params=pltpu.CompilerParams(vmem_limit_bytes=LIMIT),
    )(
        own,
        everything,
        left,
        right,
        near_column,
        near_row,
        far_column,
        far_row,
        owner,
        near_blocks,
        far_left,
        far_right,
    )


def collect_image(rows, columns, far_ref, near_ref, landed, image, send_sem, recv_sem):
    row, column = lax.axis_index("row"), lax.axis_index("col")
    copies = []
    for k in range(1, columns):
        peer = lax.rem(column + k, columns)
        copies.append(
            pltpu.make_async_remote_copy(
                src_ref=far_ref.at[peer],
                dst_ref=landed.at[column],
                send_sem=send_sem.at[k],
                recv_sem=recv_sem.at[k],
                device_id=(row, peer),
                device_id_type=MESH,
            )
        )
        copies[-1].start()
    image[...] = near_ref[...] + far_ref[column]
    for k in range(1, columns):
        source = lax.rem(column + columns - k, columns)
        pltpu.make_async_remote_copy(
            src_ref=far_ref.at[source],
            dst_ref=landed.at[source],
            send_sem=send_sem.at[k],
            recv_sem=recv_sem.at[k],
            device_id=(row, source),
            device_id_type=MESH,
        ).wait_recv()
        image[...] += landed[source]
    for copy in copies:
        copy.wait_send()


def all_sum(rows, columns, pairs, mine, parts, send_sem, recv_sem):
    count = rows * columns
    me = lax.axis_index("row") * columns + lax.axis_index("col")
    mine[...] = jnp.zeros(mine.shape, jnp.float32)
    place = 0
    for left, right in pairs:
        for s in range(left.shape[1] // LANES):
            here = slice(s * LANES, (s + 1) * LANES)
            mine[place : place + 1] = jnp.sum(left[:, here] * right[:, here], axis=0, keepdims=True)
            place += 1

    def copy(k, slot, peer):
        return pltpu.make_async_remote_copy(
            src_ref=mine,
            dst_ref=parts.at[slot],
            send_sem=send_sem.at[k],
            recv_sem=recv_sem.at[k],
            device_id=coordinates(peer, columns),
            device_id_type=MESH,
        )

    @pl.loop(1, count)
    def _(k):
        copy(k, me, lax.rem(me + k, count)).start()

    parts[me] = mine[...]

    @pl.loop(1, count)
    def _(k):
        source = lax.rem(me + count - k, count)
        copy(k, source, source).wait_recv()

    @pl.loop(1, count)
    def _(k):
        copy(k, me, lax.rem(me + k, count)).wait_send()

    return jnp.sum(jnp.sum(parts[...], axis=0), axis=1, keepdims=True)


def middle_kernel(
    rows,
    columns,
    far_ref,
    near_ref,
    first_ref,
    basis_ref,
    own_ref,
    all_ref,
    left_ref,
    right_ref,
    entries_ref,
    landed,
    image,
    mine,
    parts,
    mine_two,
    parts_two,
    collect_send,
    collect_recv,
    sum_send,
    sum_recv,
    sum_send_two,
    sum_recv_two,
    spread_send,
    spread_recv,
):
    me = lax.axis_index("row") * columns + lax.axis_index("col")
    panels = rows * columns * image.shape[0] * LANES
    sides = image.shape[1] // LANES
    lanes = [slice(s * LANES, (s + 1) * LANES) for s in range(sides)]
    enter(me, rows, columns)
    collect_image(rows, columns, far_ref, near_ref, landed, image, collect_send, collect_recv)
    project = (
        all_sum(rows, columns, [(first_ref, image)], mine, parts, sum_send, sum_recv) / panels
    )
    for s in range(sides):
        image[:, lanes[s]] = image[:, lanes[s]] - project[s : s + 1] * first_ref[:, lanes[s]]
    norm = jnp.sqrt(
        all_sum(
            rows, columns, [(image, image)], mine_two, parts_two, sum_send_two, sum_recv_two
        )
        / panels
        + epsilon
    )
    for s in range(sides):
        value = image[:, lanes[s]] / norm[s : s + 1]
        basis_ref[:, lanes[s]] = value
        own_ref[:, lanes[s]] = value.astype(jnp.bfloat16)
    entries_ref[0] = jnp.broadcast_to(project, mine.shape)
    entries_ref[1] = jnp.broadcast_to(norm, mine.shape)
    spread_densities(rows, columns, own_ref, all_ref, left_ref, right_ref, spread_send, spread_recv)


def middle(far, near, first, rows, columns, collective_id):
    blocks, width = near.shape
    count = rows * columns
    dma = pltpu.SemaphoreType.DMA
    return pl.pallas_call(
        functools.partial(middle_kernel, rows, columns),
        out_shape=[
            jax.ShapeDtypeStruct(near.shape, jnp.float32),
            jax.ShapeDtypeStruct(near.shape, jnp.bfloat16),
            *density_shapes(blocks, width, rows),
            jax.ShapeDtypeStruct((2, 8, LANES), jnp.float32),
        ],
        in_specs=[VMEM] * 3,
        out_specs=[VMEM] * 6,
        scratch_shapes=[
            pltpu.VMEM((columns, blocks, width), jnp.float32),
            pltpu.VMEM((blocks, width), jnp.float32),
            pltpu.VMEM((8, LANES), jnp.float32),
            pltpu.VMEM((count, 8, LANES), jnp.float32),
            pltpu.VMEM((8, LANES), jnp.float32),
            pltpu.VMEM((count, 8, LANES), jnp.float32),
            dma((columns,)),
            dma((columns,)),
            dma((count,)),
            dma((count,)),
            dma((count,)),
            dma((count,)),
            dma((rows + 1,)),
            dma((rows + 1,)),
        ],
        compiler_params=pltpu.CompilerParams(
            collective_id=collective_id, has_side_effects=True, vmem_limit_bytes=LIMIT
        ),
    )(far, near, first)


def last_kernel(
    rows,
    columns,
    far_ref,
    near_ref,
    first_ref,
    basis_ref,
    next_ref,
    entries_ref,
    landed,
    image,
    mine,
    parts,
    collect_send,
    collect_recv,
    sum_send,
    sum_recv,
):
    me = lax.axis_index("row") * columns + lax.axis_index("col")
    panels = rows * columns * image.shape[0] * LANES
    sides = image.shape[1] // LANES
    enter(me, rows, columns)
    collect_image(rows, columns, far_ref, near_ref, landed, image, collect_send, collect_recv)
    project = (
        all_sum(
            rows,
            columns,
            [(first_ref, image), (basis_ref, image)],
            mine,
            parts,
            sum_send,
            sum_recv,
        )
        / panels
    )
    for s in range(sides):
        here = slice(s * LANES, (s + 1) * LANES)
        next_ref[:, here] = (
            image[:, here]
            - project[s : s + 1] * first_ref[:, here]
            - project[sides + s : sides + s + 1] * basis_ref[:, here]
        )
    entries_ref[...] = jnp.broadcast_to(project, mine.shape)


def last(far, near, first, basis, rows, columns, collective_id):
    blocks, width = near.shape
    count = rows * columns
    dma = pltpu.SemaphoreType.DMA
    return pl.pallas_call(
        functools.partial(last_kernel, rows, columns),
        out_shape=[
            jax.ShapeDtypeStruct(near.shape, jnp.float32),
            jax.ShapeDtypeStruct((8, LANES), jnp.float32),
        ],
        in_specs=[VMEM] * 4,
        out_specs=[VMEM] * 2,
        scratch_shapes=[
            pltpu.VMEM((columns, blocks, width), jnp.float32),
            pltpu.VMEM((blocks, width), jnp.float32),
            pltpu.VMEM((8, LANES), jnp.float32),
            pltpu.VMEM((count, 8, LANES), jnp.float32),
            dma((columns,)),
            dma((columns,)),
            dma((count,)),
            dma((count,)),
        ],
        compiler_params=pltpu.CompilerParams(
            collective_id=collective_id, has_side_effects=True, vmem_limit_bytes=LIMIT
        ),
    )(far, near, first, basis)


def body(
    right_side,
    cluster_of,
    near_rows,
    near_columns,
    near_blocks,
    far_rows,
    far_columns,
    far_rank,
    far_left,
    far_right,
):
    rows = lax.axis_size("row")
    columns = lax.axis_size("col")
    count = rows * columns
    blocks, sides, lanes = right_side.shape
    width = sides * lanes
    capacity = 2 * blocks // count
    panels = blocks * count * lanes
    rank = far_left.shape[1]
    far_count = far_rows.shape[0] // columns
    near_count = near_rows.shape[0] // columns
    chunk = 32

    target = cluster_of // blocks
    place = cluster_of % blocks
    order = jnp.arange(blocks, dtype=jnp.int32)
    earlier = (target[None, :] == target[:, None]) & (order[None, :] < order[:, None])
    slot = target * capacity + jnp.sum(earlier.astype(jnp.int32), axis=1)
    slots = count * capacity
    to_slot = slot[None, :] == jnp.arange(slots, dtype=jnp.int32)[:, None]
    to_slot_f = to_slot.astype(jnp.float32)
    marks = jnp.sum(jnp.where(to_slot, place[None, :] + 1, 0), axis=1).astype(jnp.float32)

    lane = jnp.arange(lanes, dtype=jnp.int32)
    squares = jnp.sum(right_side * right_side, axis=(0, 2))
    half = lanes // 2
    step = half // sides
    square_lanes = jnp.repeat(squares, step)
    extra = jnp.concatenate(
        [
            jnp.broadcast_to(marks[:, None], (slots, half)),
            jnp.broadcast_to(square_lanes[None, :], (slots, half)),
        ],
        axis=1,
    )
    outgoing = jnp.dot(to_slot_f, right_side.reshape(blocks, width), precision=HIGH)
    arrived = exchange(
        jnp.concatenate([outgoing, extra], axis=1).reshape(count, capacity, width + lanes),
        rows,
        columns,
        0,
    )
    total = jnp.sum(arrived[:, 0, width + half :], axis=0).reshape(sides, step)[:, 0]
    side_norm = jnp.sqrt(total / panels + epsilon)
    arrived = arrived.reshape(slots, width + lanes)
    held = arrived[:, width].astype(jnp.int32) - 1
    from_slot = held[None, :] == order[:, None]
    to_cluster = from_slot.astype(jnp.float32)
    norm_lanes = jnp.repeat(side_norm, lanes)
    first = jnp.dot(to_cluster, arrived[:, :width], precision=HIGH) / norm_lanes[None, :]

    group = jnp.arange(columns, dtype=jnp.int32)[:, None]
    entry_rank = jnp.arange(rank, dtype=jnp.int32)
    owner = jnp.where(
        entry_rank[None, :] < far_rank[:, None],
        (jnp.arange(far_rank.shape[0], dtype=jnp.int32) % chunk)[:, None],
        -1,
    ).reshape(columns, far_count // chunk, chunk * rank)
    tables = (
        near_columns[:, None],
        near_rows.reshape(columns, 1, near_count),
        far_columns[:, None],
        (far_rows.reshape(columns, far_count) - group * blocks).reshape(columns, 1, far_count),
        owner,
    )
    own = first.astype(jnp.bfloat16)
    densities = spread(own, rows, columns, 1)
    near, far = operate(densities, own, tables, near_blocks, far_left, far_right, sides, columns)
    basis, own, *densities, entries = middle(far, near, first, rows, columns, 2)
    near, far = operate(densities, own, tables, near_blocks, far_left, far_right, sides, columns)
    following, entries_two = last(far, near, first, basis, rows, columns, 3)

    results = jnp.concatenate([basis, following], axis=1)
    returned = exchange(
        jnp.dot(to_cluster.T, results, precision=HIGH).reshape(count, capacity, 2 * width),
        rows,
        columns,
        4,
    )
    results = jnp.dot(to_slot_f.T, returned.reshape(slots, 2 * width), precision=HIGH)
    second_basis = results[:, :width].reshape(blocks, sides, lanes)
    next_vector = results[:, width:].reshape(blocks, sides, lanes)
    hessenberg = jnp.concatenate(
        [
            side_norm[None, :],
            entries[:, :sides, 0],
            entries_two[: 2 * sides, 0].reshape(2, sides),
        ],
        axis=0,
    )
    return (second_basis, next_vector, hessenberg)


def solution(mesh):
    vector = P(("row", "col"), None, None)
    table = P(("row", "col"))
    placed = (vector, table, table, table, vector, table, table, table, vector, vector)
    return jax.shard_map(
        body,
        mesh=mesh,
        in_specs=placed,
        out_specs=(vector, vector, P()),
        check_vma=False,
    )
```

time: 652 us -> 233 us (0.36)
  the two profiles are of different devices: /device:TPU:0 before, /device:TPU:15 now
where the time goes in v1:
time: 233 us; the launch traced here: 232 us
  Pallas kernels  205 us (88%)
  local copies, waits for them, and re-layouts  10.8 us (5%)
  matrix products  7.78 us (3%)
  other arithmetic  7.25 us (3%)
    pallas_call x1, Pallas kernels, middle(): pl.pallas_call(functools.partial(middle_kernel, rows, columns), out_shape...  56.7 us
    pallas_call x2, Pallas kernels, exchange(): pl.pallas_call(functools.partial(exchange_kernel, rows, columns), out_sha...  54.4 us
    pallas_call x2, Pallas kernels, operate(): pl.pallas_call(functools.partial(operator_kernel, sides), grid=(groups,),...  40.8 us
    pallas_call x1, Pallas kernels, last(): pl.pallas_call(functools.partial(last_kernel, rows, columns), out_shape=[...  36 us
    pallas_call x1, Pallas kernels, spread(): pl.pallas_call(functools.partial(spread_kernel, rows, columns), out_shape...  17.3 us

profile of v1, /device:TPU:15, one launch (start us, length us, event | category | flops | bytes accessed | tf_op | source)
XLA Modules:
  0.0 231.8 jit_solution(637586351223940482)
XLA Ops:
  0.6 1.2 multiply_reduce_fusion
  1.8 0.7 and_select_fusion.1
  2.5 0.2 convert_reduce_fusion
  2.7 0.1 select_reduce_fusion
  2.8 0.1 broadcast_in_dim.68
  2.9 0.1 reshape.147
  3.0 1.4 broadcast_subtract_fusion.far_row_ref
  4.3 0.1 pad.7.clone
  4.4 1.4 reshape.137.near_row_ref
  5.8 0.8 lt.54
  6.6 0.1 lt.52
  6.6 0.1 broadcast_in_dim.67
  6.7 1.5 broadcast_in_dim.77.near_column_ref
  8.2 0.2 broadcast_in_dim.74
  8.4 0.3 broadcast_in_dim.75
  8.7 0.2 lt.55
  8.9 0.3 lt.56
  9.2 0.7 copy_select_fusion.owner_ref
  9.9 1.7 copy.36.far_column_ref
  11.6 1.3 fusion.6
  12.9 0.9 maximum_bitcast_fusion.send_ref
  13.8 22.7 %shard_map.121 = f32[32,8,640]{2,1,0:T(8,128)} custom-call(f32[32,8,640]{2,1,0:T(8,128)} %maximum_bitcast_fusion.send_ref), custom_call_target="tpu_custom_call" | custom-call | tf_op jit(solution)/shard_map/pallas_call | solution.py:82
  36.6 1.0 slice_reduce_fusion
  37.6 0.1 reshape.136
  37.7 0.1 sqrt_reduce_fusion
  37.8 0.1 broadcast_bitcast_fusion
  37.9 0.9 convert_add_fusion
  38.8 0.1 copy.42
  38.9 2.1 fusion.20
  41.0 17.3 %shard_map.122 = (bf16[4,128,512]{2,1,0:T(8,128)(2,1)}, bf16[32,512]{1,0:T(8,128)(2,1)}, bf16[32,512]{1,0:T(8,128)(2,1)}) custom-call(bf16[128,512]{1,0:T(8,128)(2,1)} %get-tuple-element.49.own_ref), custom_call_target="tpu_custom_call" | custom-call | tf_op jit(solution)/shard_map/pallas_call | solution.py:170
  58.4 20.4 %shard_map.123 = (f32[128,512]{1,0:T(8,128)}, f32[8,128,512]{2,1,0:T(8,128)}) custom-call(bf16[128,512]{1,0:T(8,128)(2,1)} %get-tuple-element.49.own_ref, bf16[4,128,512]{2,1,0:T(8,128)(2,1)} %get-tuple-element.18.all_ref, bf16[32,512]{1,0:T(8,128)(2,1)} %get-tuple-element.19.left_ref, bf16[32,512]{1,0:T(8,128)(2,1)} %get-tuple-element.20.right_ref, ...), custom_call_target="tpu_custom_call" | custom-call | tf_op jit(solution)/shard_map/pallas_call | solution.py:306
  78.7 56.7 %shard_map.124 = (f32[128,512]{1,0:T(8,128)}, bf16[128,512]{1,0:T(8,128)(2,1)}, bf16[4,128,512]{2,1,0:T(8,128)(2,1)}, bf16[32,512]{1,0:T(8,128)(2,1)}, bf16[32,512]{1,0:T(8,128)(2,1)}, /*index=5*/f32[2,8,128]{2,1,0:T(8,128)}) custom-call(f32[8,128,512]{2,1,0:T(8,128)} %get-tuple-element.21.far_ref, f32[128,512]{1,0:T(8,128)} %get-tuple-element.22.near_ref, ...), custom_call_target="tpu_custom_call" | custom-call | tf_op jit(solution)/shard_map/pallas_call | solution.py:484
  135.4 0.8 slice_reduce_fusion.2
  136.2 0.0 copy-start
  136.2 20.4 %shard_map.125 = (f32[128,512]{1,0:T(8,128)}, f32[8,128,512]{2,1,0:T(8,128)}) custom-call(bf16[128,512]{1,0:T(8,128)(2,1)} %get-tuple-element.24.own_ref, bf16[4,128,512]{2,1,0:T(8,128)(2,1)} %get-tuple-element.25.all_ref, bf16[32,512]{1,0:T(8,128)(2,1)} %get-tuple-element.26.left_ref, bf16[32,512]{1,0:T(8,128)(2,1)} %get-tuple-element.27.right_ref, ...), custom_call_target="tpu_custom_call" | custom-call | tf_op jit(solution)/shard_map/pallas_call | solution.py:306
  156.6 36.0 %shard_map.126 = (f32[128,512]{1,0:T(8,128)}, f32[8,128]{1,0:T(8,128)}) custom-call(f32[8,128,512]{2,1,0:T(8,128)} %get-tuple-element.28.far_ref, f32[128,512]{1,0:T(8,128)} %get-tuple-element.29.near_ref, f32[128,512]{1,0:T(8,128)} %get-tuple-element.50.first_ref, f32[128,512]{1,0:T(8,128)} %get-tuple-element.23.basis_ref), custom_call_target="tpu_custom_call" | custom-call | tf_op jit(solution)/shard_map/pallas_call | solution.py:565
  192.6 0.8 slice_reduce_fusion.1
  193.4 0.1 reshape_squeeze.3
  193.5 0.7 copy.39
  194.1 0.0 copy-done
  194.1 2.6 %convolution_bitcast_fusion.send_ref = f32[32,8,1024]{2,1,0:T(8,128)} fusion(f32[128,512]{1,0:T(8,128)} %get-tuple-element.30, f32[128,512]{1,0:T(8,128)S(1)} %copy-done, s32[256]{0:T(256)S(1)} %bitcast.33), kind=kOutput, calls=%fused_computation | convolution fusion | flops 402817024 | bytes 1573888 | tf_op jit(solution)/shard_map/dot_general | solution.py:674
  196.7 31.7 %shard_map.127 = f32[32,8,1024]{2,1,0:T(8,128)} custom-call(f32[32,8,1024]{2,1,0:T(8,128)} %convolution_bitcast_fusion.send_ref), custom_call_target="tpu_custom_call" | custom-call | tf_op jit(solution)/shard_map/pallas_call | solution.py:82
  228.4 1.7 fusion
  230.2 0.8 reshape.142
  231.0 0.8 reshape.141
  (8 shorter events, 0.1 us)
Async XLA Ops:
  136.2 58.0 %copy-start = (f32[128,512]{1,0:T(8,128)S(1)}, f32[128,512]{1,0:T(8,128)}, u32[]{:S(2)}) copy-start(f32[128,512]{1,0:T(8,128)} %get-tuple-element.23.basis_ref) | copy-start | bytes 786436

commit v2 on v0

v2 whole, which is shorter than its diff:
```python
import functools

import jax
import jax.numpy as jnp
from jax import lax
from jax.experimental import pallas as pl
from jax.experimental.pallas import tpu as pltpu
from jax.sharding import PartitionSpec as P

epsilon = 1e-06
MESH = pl.DeviceIdType.MESH
HIGH = lax.Precision.HIGHEST
VMEM = pl.BlockSpec(memory_space=pltpu.VMEM)
LANES = 128
LIMIT = 56 * 2**20


def coordinates(index, column_count):
    return (lax.div(index, column_count), lax.rem(index, column_count))


def enter(me, rows, columns):
    count = rows * columns
    barrier = pltpu.get_barrier_semaphore()

    @pl.loop(1, count)
    def _(k):
        pl.semaphore_signal(
            barrier,
            inc=1,
            device_id=coordinates(lax.rem(me + k, count), columns),
            device_id_type=MESH,
        )

    pl.semaphore_wait(barrier, count - 1)


def exchange_kernel(rows, columns, send_ref, recv_ref, send_sem, recv_sem):
    count = rows * columns
    me = lax.axis_index("row") * columns + lax.axis_index("col")
    enter(me, rows, columns)

    def copy(k):
        peer = lax.rem(me + k, count)
        return pltpu.make_async_remote_copy(
            src_ref=send_ref.at[peer],
            dst_ref=recv_ref.at[me],
            send_sem=send_sem.at[k],
            recv_sem=recv_sem.at[k],
            device_id=coordinates(peer, columns),
            device_id_type=MESH,
        )

    def arrival(k):
        source = lax.rem(me + count - k, count)
        return pltpu.make_async_remote_copy(
            src_ref=send_ref.at[source],
            dst_ref=recv_ref.at[source],
            send_sem=send_sem.at[k],
            recv_sem=recv_sem.at[k],
            device_id=coordinates(source, columns),
            device_id_type=MESH,
        )

    @pl.loop(1, count)
    def _(k):
        copy(k).start()

    recv_ref[me] = send_ref[me]

    @pl.loop(1, count)
    def _(k):
        arrival(k).wait_recv()

    @pl.loop(1, count)
    def _(k):
        copy(k).wait_send()


def exchange(send, rows, columns, collective_id):
    count = rows * columns
    return pl.pallas_call(
        functools.partial(exchange_kernel, rows, columns),
        out_shape=jax.ShapeDtypeStruct(send.shape, send.dtype),
        in_specs=[VMEM],
        out_specs=VMEM,
        scratch_shapes=[
            pltpu.SemaphoreType.DMA((count,)),
            pltpu.SemaphoreType.DMA((count,)),
        ],
        compiler_params=pltpu.CompilerParams(
            collective_id=collective_id, has_side_effects=True, vmem_limit_bytes=LIMIT
        ),
    )(send)


def split_dot(picker, value):
    high = value.astype(jnp.bfloat16)
    rest = value - high.astype(jnp.float32)
    middle = rest.astype(jnp.bfloat16)
    low = (rest - middle.astype(jnp.float32)).astype(jnp.bfloat16)
    dot = functools.partial(jnp.dot, picker, preferred_element_type=jnp.float32)
    return dot(high) + (dot(middle) + dot(low))


def one_hot(condition):
    return jnp.where(condition, 1.0, 0.0).astype(jnp.bfloat16)


def remote(source, destination, sends, recvs, k, device):
    return pltpu.make_async_remote_copy(
        src_ref=source,
        dst_ref=destination,
        send_sem=sends.at[k],
        recv_sem=recvs.at[k],
        device_id=device,
        device_id_type=MESH,
    )


def near_group(sides, g, tables_ref, extended, near_ref, near_out, image):
    near_count = near_ref.shape[1]
    reach = extended.shape[0]
    blocks = image.shape[0]
    table = tables_ref[g]
    turned = table.T
    column = turned[:near_count, 0:1]
    pick = one_hot(
        column == lax.broadcasted_iota(jnp.int32, (near_count, reach), 1).astype(jnp.float32)
    )
    picked = jnp.dot(pick, extended[...], preferred_element_type=jnp.float32)
    batch = 8
    row_id = lax.rem(lax.broadcasted_iota(jnp.int32, (sides * batch, LANES), 0), batch)
    for j in range(near_count // batch):
        here = slice(j * batch, (j + 1) * batch)
        stacked = jnp.concatenate(
            [picked[here, s * LANES : (s + 1) * LANES] for s in range(sides)], axis=0
        ).astype(jnp.bfloat16)
        product = lax.dot_general(
            stacked,
            near_ref[g, here].reshape(batch * LANES, LANES),
            (((1,), (1,)), ((), ())),
            preferred_element_type=jnp.float32,
        )
        value = jnp.zeros((sides * batch, LANES), jnp.float32)
        for e in range(batch):
            value = jnp.where(row_id == e, product[:, e * LANES : (e + 1) * LANES], value)
        for s in range(sides):
            near_out[here, s * LANES : (s + 1) * LANES] = value[s * batch : (s + 1) * batch]
    place = one_hot(
        table[1:2, :near_count]
        == lax.broadcasted_iota(jnp.int32, (blocks, near_count), 0).astype(jnp.float32)
    )
    image[...] += split_dot(place, near_out[...])


def far_group(sides, g, tables_ref, everything, far_left, far_right, far_out):
    rows, blocks, width = everything.shape
    far_count, rank = far_left.shape[1:3]
    table = tables_ref[g]
    turned = table.T
    lanes = lax.broadcasted_iota(jnp.int32, (far_count, rows * blocks), 1).astype(jnp.float32)
    pick = one_hot(turned[:far_count, 2:3] == lanes)
    picked = jnp.dot(
        pick, everything[...].reshape(rows * blocks, width), preferred_element_type=jnp.float32
    )
    batch = 32
    shape = (sides * batch, batch * rank)
    entry = lax.rem(lax.broadcasted_iota(jnp.int32, shape, 0), batch)
    lane = lax.broadcasted_iota(jnp.int32, shape, 1)
    term = lax.rem(lane, rank).astype(jnp.float32)
    own_entry = lax.div(lane, rank) == entry
    for j in range(far_count // batch):
        here = slice(j * batch, (j + 1) * batch)
        stacked = jnp.concatenate(
            [picked[here, s * LANES : (s + 1) * LANES] for s in range(sides)], axis=0
        ).astype(jnp.bfloat16)
        product = lax.dot_general(
            stacked,
            far_right[g, here].reshape(batch * rank, LANES),
            (((1,), (1,)), ((), ())),
            preferred_element_type=jnp.float32,
        )
        ranks = jnp.concatenate([turned[here, 4:5]] * sides, axis=0)
        coefficients = jnp.where(own_entry & (term < ranks), product, 0.0).astype(jnp.bfloat16)
        value = jnp.dot(
            coefficients,
            far_left[g, here].reshape(batch * rank, LANES),
            preferred_element_type=jnp.float32,
        )
        for s in range(sides):
            far_out[here, s * LANES : (s + 1) * LANES] = value[s * batch : (s + 1) * batch]
    place = one_hot(
        table[3:4, :far_count]
        == lax.broadcasted_iota(jnp.int32, (blocks, far_count), 0).astype(jnp.float32)
    )
    return split_dot(place, far_out[...])


def arnoldi_kernel(
    rows,
    columns,
    first_ref,
    tables_ref,
    to_mesh_ref,
    near_hbm,
    far_left_hbm,
    far_right_hbm,
    basis_back_ref,
    image_back_ref,
    entries_ref,
    entries_two_ref,
    near_ref,
    far_left,
    far_right,
    own,
    basis,
    image,
    everything,
    extended,
    left,
    right,
    near_out,
    far_out,
    to_partner,
    from_partner,
    to_chips,
    from_chips,
    outgoing,
    outgoing_two,
    mine,
    parts,
    load_sem,
    halo_send,
    halo_recv,
    spread_send,
    spread_recv,
    pair_send,
    pair_recv,
    chip_send,
    chip_recv,
    sum_send,
    sum_recv,
    back_send,
    back_recv,
):
    row, column = lax.axis_index("row"), lax.axis_index("col")
    count = rows * columns
    me = row * columns + column
    blocks, width = first_ref.shape
    sides = width // LANES
    halo = left.shape[0]
    groups = near_ref.shape[0]
    pairs = columns // 2
    chip, core = lax.div(column, 2), lax.rem(column, 2)
    partner = 2 * chip + 1 - core
    panels = count * blocks * LANES
    lanes = [slice(s * LANES, (s + 1) * LANES) for s in range(sides)]
    capacity = outgoing.shape[1]

    def load(kind, g):
        source, target = (
            (near_hbm, near_ref),
            (far_left_hbm, far_left),
            (far_right_hbm, far_right),
        )[kind]
        return pltpu.make_async_copy(source.at[g], target.at[g], load_sem.at[kind, g])

    for kind in range(3):

        @pl.loop(0, groups)
        def _(g, kind=kind):
            load(kind, g).start()

    enter(me, rows, columns)

    def operate(a, between):
        after = coordinates(lax.rem(me + 1, count), columns)
        before = coordinates(lax.rem(me + count - 1, count), columns)
        halos = [
            remote(
                own.at[pl.ds(blocks - halo, halo)],
                left,
                halo_send.at[a],
                halo_recv.at[a],
                0,
                after,
            ),
            remote(own.at[pl.ds(0, halo)], right, halo_send.at[a], halo_recv.at[a], 1, before),
        ]
        for copy in halos:
            copy.start()
        copies = [
            remote(
                own,
                everything.at[row],
                spread_send.at[a],
                spread_recv.at[a],
                k,
                (lax.rem(row + k, rows), column),
            )
            for k in range(1, rows)
        ]
        for copy in copies:
            copy.start()
        everything[row] = own[...]
        image[...] = 0.5 * own[...].astype(jnp.float32)
        extended[halo : halo + blocks] = own[...]
        for copy in halos:
            copy.wait()
        extended[0:halo] = left[...]
        extended[halo + blocks :] = right[...]

        @pl.loop(0, groups)
        def _(g):
            if a == 0:
                load(0, g).wait()
            near_group(sides, g, tables_ref, extended, near_ref, near_out, image)

        for k in range(1, rows):
            source = lax.rem(row + rows - k, rows)
            remote(
                own,
                everything.at[source],
                spread_send.at[a],
                spread_recv.at[a],
                k,
                (source, column),
            ).wait_recv()
        for copy in copies:
            copy.wait_send()
        between()
        if a == 0:
            for kind in (1, 2):

                @pl.loop(0, groups)
                def _(g, kind=kind):
                    load(kind, g).wait()

        far = functools.partial(
            far_group,
            sides,
            tables_ref=tables_ref,
            everything=everything,
            far_left=far_left,
            far_right=far_right,
            far_out=far_out,
        )

        def pair_copy(k, q):
            return remote(
                to_partner.at[q],
                from_partner.at[q],
                pair_send.at[a],
                pair_recv.at[a],
                k,
                (row, partner),
            )

        def chip_copy(k, q):
            return remote(
                to_chips.at[q],
                from_chips.at[chip],
                chip_send.at[a],
                chip_recv.at[a],
                k,
                (row, 2 * q + core),
            )

        @pl.loop(1, pairs + 1)
        def _(i):
            q = lax.rem(chip + i, pairs)
            k = i - 1
            to_partner[q] = far(2 * q + 1 - core)
            pair_copy(k, q).start()
            to_chips[q] = far(2 * q + core)
            pair_copy(k, q).wait_recv()
            to_chips[q] = to_chips[q] + from_partner[q]

            @pl.when(i < pairs)
            def _():
                chip_copy(k, q).start()

        image[...] += to_chips[chip]
        for i in range(1, pairs):
            source = lax.rem(chip + pairs - i, pairs)
            remote(
                to_chips.at[source],
                from_chips.at[source],
                chip_send.at[a],
                chip_recv.at[a],
                i - 1,
                (row, 2 * source + core),
            ).wait_recv()
            image[...] += from_chips[source]
        for i in range(1, pairs + 1):
            q = lax.rem(chip + i, pairs)
            pair_copy(i - 1, q).wait_send()
            if i < pairs:
                chip_copy(i - 1, q).wait_send()

    def all_sum(n, pairings):
        place = 0
        mine[n] = jnp.zeros(mine.shape[1:], jnp.float32)
        for one, two in pairings:
            for here in lanes:
                mine[n, place : place + 1] = jnp.sum(
                    one[:, here] * two[:, here], axis=0, keepdims=True
                )
                place += 1

        def copy(k, slot, peer):
            return remote(
                mine.at[n],
                parts.at[n, slot],
                sum_send.at[n],
                sum_recv.at[n],
                k,
                coordinates(peer, columns),
            )

        @pl.loop(1, count)
        def _(k):
            copy(k, me, lax.rem(me + k, count)).start()

        parts[n, me] = mine[n]

        @pl.loop(1, count)
        def _(k):
            source = lax.rem(me + count - k, count)
            copy(k, source, source).wait_recv()

        @pl.loop(1, count)
        def _(k):
            copy(k, me, lax.rem(me + k, count)).wait_send()

        return jnp.sum(jnp.sum(parts[n], axis=0), axis=1, keepdims=True) / panels

    def back(n, sent, landed):
        def copy(k, peer, slot):
            return remote(
                sent.at[peer],
                landed.at[slot],
                back_send.at[n],
                back_recv.at[n],
                k,
                coordinates(peer, columns),
            )

        def start(value):
            picked = split_dot(to_mesh_ref[...], value[...])
            for d in range(count):
                sent[d] = picked[d * capacity : (d + 1) * capacity]

            @pl.loop(1, count)
            def _(k):
                copy(k, lax.rem(me + k, count), me).start()

            landed[me] = sent[me]

        def wait():
            @pl.loop(1, count)
            def _(k):
                source = lax.rem(me + count - k, count)
                copy(k, source, source).wait_recv()

            @pl.loop(1, count)
            def _(k):
                copy(k, lax.rem(me + k, count), me).wait_send()

        return start, wait

    basis_start, basis_wait = back(0, outgoing, basis_back_ref)
    image_start, image_wait = back(1, outgoing_two, image_back_ref)

    own[...] = first_ref[...].astype(jnp.bfloat16)
    operate(0, lambda: None)
    project = all_sum(0, [(first_ref, image)])
    for s in range(sides):
        image[:, lanes[s]] = image[:, lanes[s]] - project[s : s + 1] * first_ref[:, lanes[s]]
    norm = jnp.sqrt(all_sum(1, [(image, image)]) + epsilon)
    for s in range(sides):
        value = image[:, lanes[s]] / norm[s : s + 1]
        basis[:, lanes[s]] = value
        own[:, lanes[s]] = value.astype(jnp.bfloat16)
    entries_ref[0] = jnp.broadcast_to(project, mine.shape[1:])
    entries_ref[1] = jnp.broadcast_to(norm, mine.shape[1:])
    operate(1, lambda: basis_start(basis))
    image_start(image)
    projects = all_sum(2, [(first_ref, image), (basis, image)])
    entries_two_ref[...] = jnp.broadcast_to(projects, mine.shape[1:])
    basis_wait()
    image_wait()


def arnoldi(first, tables, to_mesh, near_blocks, far_left, far_right, rows, columns, capacity):
    blocks, width = first.shape
    count = rows * columns
    groups = columns
    near_blocks = near_blocks.reshape(groups, -1, *near_blocks.shape[1:])
    far_left = far_left.reshape(groups, -1, *far_left.shape[1:])
    far_right = far_right.reshape(groups, -1, *far_right.shape[1:])
    halo = blocks // 4
    pairs = columns // 2
    dma = pltpu.SemaphoreType.DMA
    real, half = jnp.float32, jnp.bfloat16
    slots = (count, capacity, width)
    hbm = pl.BlockSpec(memory_space=pl.ANY)
    return pl.pallas_call(
        functools.partial(arnoldi_kernel, rows, columns),
        out_shape=[
            jax.ShapeDtypeStruct(slots, real),
            jax.ShapeDtypeStruct(slots, real),
            jax.ShapeDtypeStruct((2, 8, LANES), real),
            jax.ShapeDtypeStruct((8, LANES), real),
        ],
        in_specs=[VMEM] * 3 + [hbm] * 3,
        out_specs=[VMEM] * 4,
        scratch_shapes=[
            pltpu.VMEM(near_blocks.shape, half),
            pltpu.VMEM(far_left.shape, half),
            pltpu.VMEM(far_right.shape, half),
            pltpu.VMEM((blocks, width), half),
            pltpu.VMEM((blocks, width), real),
            pltpu.VMEM((blocks, width), real),
            pltpu.VMEM((rows, blocks, width), half),
            pltpu.VMEM((blocks + 2 * halo, width), half),
            pltpu.VMEM((halo, width), half),
            pltpu.VMEM((halo, width), half),
            pltpu.VMEM((near_blocks.shape[1], width), real),
            pltpu.VMEM((far_left.shape[1], width), real),
            pltpu.VMEM((pairs, blocks, width), real),
            pltpu.VMEM((pairs, blocks, width), real),
            pltpu.VMEM((pairs, blocks, width), real),
            pltpu.VMEM((pairs, blocks, width), real),
            pltpu.VMEM(slots, real),
            pltpu.VMEM(slots, real),
            pltpu.VMEM((3, 8, LANES), real),
            pltpu.VMEM((3, count, 8, LANES), real),
            dma((3, groups)),
            dma((2, 2)),
            dma((2, 2)),
            dma((2, rows)),
            dma((2, rows)),
            dma((2, pairs)),
            dma((2, pairs)),
            dma((2, pairs)),
            dma((2, pairs)),
            dma((3, count)),
            dma((3, count)),
            dma((2, count)),
            dma((2, count)),
        ],
        compiler_params=pltpu.CompilerParams(
            collective_id=1, has_side_effects=True, vmem_limit_bytes=LIMIT
        ),
    )(first, tables, to_mesh, near_blocks, far_left, far_right)


def body(
    right_side,
    cluster_of,
    near_rows,
    near_columns,
    near_blocks,
    far_rows,
    far_columns,
    far_rank,
    far_left,
    far_right,
):
    rows = lax.axis_size("row")
    columns = lax.axis_size("col")
    count = rows * columns
    blocks, sides, lanes = right_side.shape
    width = sides * lanes
    capacity = 2 * blocks // count
    panels = blocks * count * lanes
    far_count = far_rows.shape[0] // columns

    target = cluster_of // blocks
    place = cluster_of % blocks
    order = jnp.arange(blocks, dtype=jnp.int32)
    earlier = (target[None, :] == target[:, None]) & (order[None, :] < order[:, None])
    slot = target * capacity + jnp.sum(earlier.astype(jnp.int32), axis=1)
    slots = count * capacity
    to_slot = slot[None, :] == jnp.arange(slots, dtype=jnp.int32)[:, None]
    to_slot_f = to_slot.astype(jnp.float32)
    marks = jnp.sum(jnp.where(to_slot, place[None, :] + 1, 0), axis=1).astype(jnp.float32)

    lane = jnp.arange(lanes, dtype=jnp.int32)
    squares = jnp.sum(right_side * right_side, axis=(0, 2))
    half = lanes // 2
    step = half // sides
    square_lanes = jnp.repeat(squares, step)
    extra = jnp.concatenate(
        [
            jnp.broadcast_to(marks[:, None], (slots, half)),
            jnp.broadcast_to(square_lanes[None, :], (slots, half)),
        ],
        axis=1,
    )
    outgoing = jnp.dot(to_slot_f, right_side.reshape(blocks, width), precision=HIGH)
    arrived = exchange(
        jnp.concatenate([outgoing, extra], axis=1).reshape(count, capacity, width + lanes),
        rows,
        columns,
        0,
    )
    total = jnp.sum(arrived[:, 0, width + half :], axis=0).reshape(sides, step)[:, 0]
    side_norm = jnp.sqrt(total / panels + epsilon)
    arrived = arrived.reshape(slots, width + lanes)
    held = arrived[:, width].astype(jnp.int32) - 1
    from_slot = held[None, :] == order[:, None]
    to_cluster = from_slot.astype(jnp.float32)
    norm_lanes = jnp.repeat(side_norm, lanes)
    first = jnp.dot(to_cluster, arrived[:, :width], precision=HIGH) / norm_lanes[None, :]


    group = jnp.arange(columns, dtype=jnp.int32)[:, None]

    def table(values):
        values = values.reshape(columns, -1)
        return jnp.pad(values, ((0, 0), (0, lanes - values.shape[1])))

    blank = jnp.zeros((columns, lanes), jnp.int32)
    tables = jnp.stack(
        [
            table(near_columns),
            table(near_rows),
            table(far_columns),
            table(far_rows.reshape(columns, far_count) - group * blocks),
            table(far_rank),
            blank,
            blank,
            blank,
        ],
        axis=1,
    ).astype(jnp.float32)
    to_mesh = (held[:, None] == order[None, :]).astype(jnp.bfloat16)
    basis_back, image_back, entries, entries_two = arnoldi(
        first, tables, to_mesh, near_blocks, far_left, far_right, rows, columns, capacity
    )
    local = to_slot_f.T
    project_two = jnp.repeat(entries_two[:sides, 0], lanes)
    project_three = jnp.repeat(entries_two[sides : 2 * sides, 0], lanes)
    basis = jnp.dot(local, basis_back.reshape(slots, width), precision=HIGH)
    image_two = jnp.dot(local, image_back.reshape(slots, width), precision=HIGH)
    mesh_first = right_side.reshape(blocks, width) / norm_lanes[None, :]
    following = image_two - project_two[None, :] * mesh_first - project_three[None, :] * basis
    second_basis = basis.reshape(blocks, sides, lanes)
    next_vector = following.reshape(blocks, sides, lanes)
    hessenberg = jnp.concatenate(
        [
            side_norm[None, :],
            entries[:, :sides, 0],
            entries_two[: 2 * sides, 0].reshape(2, sides),
        ],
        axis=0,
    )
    return (second_basis, next_vector, hessenberg)


def solution(mesh):
    vector = P(("row", "col"), None, None)
    table = P(("row", "col"))
    placed = (vector, table, table, table, vector, table, table, table, vector, vector)
    return jax.shard_map(
        body,
        mesh=mesh,
        in_specs=placed,
        out_specs=(vector, vector, P()),
        check_vma=False,
    )
```

time: 652 us -> 157 us (0.24); the launches traced: 642 us -> 156 us
  blocking collectives: 243 us -> 0 us
  other arithmetic: 170 us -> 7.26 us
  Pallas kernels: 0 us -> 134 us
  waiting for transfers between devices: 93.6 us -> 0 us
  local copies, waits for them, and re-layouts: 63.2 us -> 7.73 us
  matrix products: 35.8 us -> 6.25 us
  starting transfers between devices: 20.5 us -> 0 us
  between operations: 15.1 us -> 0.74 us
    scatter-add x4 -> x0, other arithmetic: 161 us -> none  [the longest x2 133 us: apply_clustered(): partial_value = jnp.zeros((local_blocks * column_count, sides, width), jn...]
    psum x4 -> x0, blocking collectives: 158 us -> none  [the longest x1 40.5 us: body(): lax.psum(local_inner(right_side, right_side), ('row', 'col')) / panels]
    pallas_call x0 -> x2, Pallas kernels: none -> 134 us  [the longest x1 114 us: arnoldi(): pl.pallas_call(functools.partial(arnoldi_kernel, rows, columns), out_shap...]
    unnamed x4 -> x0, waiting for transfers between devices: 84.2 us -> none
    all_to_all x3 -> x0, blocking collectives: 53 us -> none  [the longest x2 38.3 us: relay_out(): lax.all_to_all(outgoing, ('row', 'col'), split_axis=0, concat_axis=0, til...]
    scatter x5 -> x0, local copies, waits for them, and re-layouts: 41.5 us -> none  [the longest x2 20.5 us: relay_in(): outgoing = jnp.zeros((device_count, capacity, sides, width), jnp.bfloat16...]
    all_gather x2 -> x0, blocking collectives: 31.8 us -> none  [apply_clustered(): gathered = lax.all_gather(clustered, 'row', axis=0, tiled=True)]
    dot_general x4, matrix products: 35.8 us -> 6.25 us  [the longest x1 2.1 us: body(): jnp.dot(to_cluster, arrived[:, :width], precision=HIGH)]
  transfers between devices with their start and end apart: 8 -> 0, of which waited for: 5 -> 0; matrix products, arithmetic and copies ran while one was open for 7% -> 0% of each run, Pallas kernels for 0% -> 0%
where the time goes in v2:
time: 157 us; the launch traced here: 156 us
  Pallas kernels  134 us (85%)
  local copies, waits for them, and re-layouts  7.73 us (5%)
  other arithmetic  7.26 us (5%)
  matrix products  6.25 us (4%)
    pallas_call x1, Pallas kernels, arnoldi(): pl.pallas_call(functools.partial(arnoldi_kernel, rows, columns), out_shap...  114 us
    pallas_call x1, Pallas kernels, exchange(): pl.pallas_call(functools.partial(exchange_kernel, rows, columns), out_sha...  20.6 us

profile of v2, /device:TPU:0, one launch (start us, length us, event | category | flops | bytes accessed | tf_op | source)
XLA Modules:
  0.0 156.2 jit_solution(14105281401482332193)
XLA Ops:
  0.6 1.2 multiply_reduce_fusion
  1.8 0.7 and_select_fusion.1
  2.5 0.2 convert_reduce_fusion
  2.7 0.1 select_reduce_fusion
  2.8 0.1 broadcast_in_dim.29
  2.9 0.1 reshape.153
  3.0 0.1 pad.14.clone
  3.1 0.8 broadcast_subtract_fusion
  3.8 0.8 reshape.138
  4.6 0.8 reshape.137
  5.4 0.8 stack.24
  6.1 0.6 convert_element_type.30.tables_ref
  6.7 0.1 broadcast_in_dim.28
  6.8 1.3 fusion.5
  8.2 0.9 maximum_bitcast_fusion.send_ref
  9.1 20.6 %shard_map.121 = f32[32,8,640]{2,1,0:T(8,128)} custom-call(f32[32,8,640]{2,1,0:T(8,128)} %maximum_bitcast_fusion.send_ref), custom_call_target="tpu_custom_call" | custom-call | tf_op jit(solution)/shard_map/pallas_call | solution.py:82
  29.7 1.0 slice_reduce_fusion
  30.7 0.1 reshape.136
  30.8 0.1 sqrt_reduce_fusion
  30.9 0.1 broadcast_bitcast_fusion.2
  31.0 0.9 convert_add_fusion
  31.9 0.1 copy.20
  32.0 2.1 %convolution_divide_fusion.first_ref = f32[128,512]{1,0:T(8,128)} fusion(f32[256,640]{1,0:T(8,128)} %bitcast.40, f32[512]{0:T(512)S(1)} %broadcast_bitcast_fusion.2, s32[256]{0:T(256)S(1)} %bitcast.44), kind=kOutput, calls=%fused_computation.2 | convolution fusion | flops 201424896 | bytes 789504 | tf_op jit(solution)/shard_map/dot_general | solution.py:617
  34.1 0.7 fusion.9.to_mesh_ref
  34.8 0.0 copy-start
  34.8 113.6 %shard_map.122 = (f32[32,8,512]{2,1,0:T(8,128)}, f32[32,8,512]{2,1,0:T(8,128)}, f32[2,8,128]{2,1,0:T(8,128)}, f32[8,128]{1,0:T(8,128)}) custom-call(f32[128,512]{1,0:T(8,128)} %convolution_divide_fusion.first_ref, f32[8,8,128]{2,1,0:T(8,128)} %convert_element_type.30.tables_ref, bf16[256,128]{1,0:T(8,128)(2,1)} %fusion.9.to_mesh_ref, ...), custom_call_target="tpu_custom_call" | custom-call | tf_op jit(solution)/shard_map/pallas_call | solution.py:509
  148.5 1.4 fusion.3
  149.9 0.8 slice_reduce_fusion.1
  150.7 0.9 slice_reduce_fusion.4
  151.6 0.1 reshape_squeeze.3
  151.7 0.8 slice_reduce_fusion.2
  152.5 0.7 copy.17
  153.1 0.1 broadcast_bitcast_fusion
  153.2 0.0 copy-done
  153.2 1.4 fusion
  154.6 0.8 reshape.144
  155.4 0.8 reshape.146
  (8 shorter events, 0.0 us)
Async XLA Ops:
  34.8 118.4 %copy-start = (f32[128,4,128]{2,1,0:T(4,128)S(1)}, f32[128,4,128]{2,1,0:T(4,128)}, u32[]{:S(2)}) copy-start(f32[128,4,128]{2,1,0:T(4,128)} %param.10) | copy-start | bytes 786436

commit v3 on v2

--- a/solution.py
+++ b/solution.py
@@ -201,15 +201,24 @@
     rows,
     columns,
     first_ref,
-    tables_ref,
+    near_columns_ref,
+    near_rows_ref,
+    far_columns_ref,
+    far_rows_ref,
+    far_rank_ref,
     to_mesh_ref,
+    to_own_ref,
+    mesh_first_ref,
     near_hbm,
     far_left_hbm,
     far_right_hbm,
+    basis_ref,
+    next_ref,
+    entries_ref,
+    tables_ref,
     basis_back_ref,
     image_back_ref,
-    entries_ref,
-    entries_two_ref,
+    flat,
     near_ref,
     far_left,
     far_right,
@@ -272,6 +281,15 @@
         def _(g, kind=kind):
             load(kind, g).start()
 
+    tables_ref[...] = jnp.zeros(tables_ref.shape, jnp.float32)
+    for g in range(groups):
+        for place, source in enumerate(
+            (near_columns_ref, near_rows_ref, far_columns_ref, far_rows_ref, far_rank_ref)
+        ):
+            value = source[g : g + 1]
+            if source is far_rows_ref:
+                value = value - g * blocks
+            tables_ref[g, place : place + 1, : source.shape[1]] = value.astype(jnp.float32)
     enter(me, rows, columns)
 
     def operate(a, between):
@@ -290,20 +308,39 @@
         ]
         for copy in halos:
             copy.start()
-        copies = [
-            remote(
-                own,
-                everything.at[row],
-                spread_send.at[a],
-                spread_recv.at[a],
-                k,
-                (lax.rem(row + k, rows), column),
+        everything[row] = own[...]
+
+        def inside(index):
+            return (index >= 0) & (index < rows)
+
+        def hop(way, distance, slot):
+            sign = 1 - 2 * way
+            return remote(
+                everything.at[slot],
+                everything.at[slot],
+                spread_send.at[a, way],
+                spread_recv.at[a, way],
+                distance,
+                (lax.rem(row + sign + rows, rows), column),
             )
-            for k in range(1, rows)
-        ]
-        for copy in copies:
-            copy.start()
-        everything[row] = own[...]
+
+        def relay(distance):
+            for way in range(2):
+                sign = 1 - 2 * way
+                source = row - sign * distance
+                if distance > 0:
+
+                    @pl.when(inside(source))
+                    def _(way=way, source=source):
+                        hop(way, distance - 1, source).wait_recv()
+
+                if distance < rows - 1:
+
+                    @pl.when(inside(source) & inside(row + sign))
+                    def _(way=way, source=source):
+                        hop(way, distance, source).start()
+
+        relay(0)
         image[...] = 0.5 * own[...].astype(jnp.float32)
         extended[halo : halo + blocks] = own[...]
         for copy in halos:
@@ -316,19 +353,22 @@
             if a == 0:
                 load(0, g).wait()
             near_group(sides, g, tables_ref, extended, near_ref, near_out, image)
-
-        for k in range(1, rows):
-            source = lax.rem(row + rows - k, rows)
-            remote(
-                own,
-                everything.at[source],
-                spread_send.at[a],
-                spread_recv.at[a],
-                k,
-                (source, column),
-            ).wait_recv()
-        for copy in copies:
-            copy.wait_send()
+            for distance in range(1, rows - 1):
+
+                @pl.when(g == distance * groups // (rows - 1))
+                def _(distance=distance):
+                    relay(distance)
+
+        relay(rows - 1)
+        for way in range(2):
+            sign = 1 - 2 * way
+            for distance in range(rows - 1):
+                source = row - sign * distance
+
+                @pl.when(inside(source) & inside(row + sign))
+                def _(way=way, source=source, distance=distance):
+                    hop(way, distance, source).wait_send()
+
         between()
         if a == 0:
             for kind in (1, 2):
@@ -483,17 +523,48 @@
         value = image[:, lanes[s]] / norm[s : s + 1]
         basis[:, lanes[s]] = value
         own[:, lanes[s]] = value.astype(jnp.bfloat16)
-    entries_ref[0] = jnp.broadcast_to(project, mine.shape[1:])
-    entries_ref[1] = jnp.broadcast_to(norm, mine.shape[1:])
     operate(1, lambda: basis_start(basis))
     image_start(image)
     projects = all_sum(2, [(first_ref, image), (basis, image)])
-    entries_two_ref[...] = jnp.broadcast_to(projects, mine.shape[1:])
+
+    def by_lane(column):
+        shape = (column.shape[0], LANES)
+        diagonal = lax.broadcasted_iota(jnp.int32, shape, 0) == lax.broadcasted_iota(
+            jnp.int32, shape, 1
+        )
+        return jnp.sum(jnp.where(diagonal, column, 0.0), axis=0, keepdims=True)
+
+    entries_ref[...] = jnp.zeros(entries_ref.shape, jnp.float32)
+    found = (
+        project[:sides],
+        norm[:sides],
+        projects[:sides],
+        projects[sides : 2 * sides],
+    )
+    for place, value in enumerate(found):
+        entries_ref[place : place + 1] = by_lane(value)
+
+    def home(landed):
+        for d in range(count):
+            flat[d * capacity : (d + 1) * capacity] = landed[d]
+        return split_dot(to_own_ref[...], flat[...])
+
     basis_wait()
+    basis_ref[...] = home(basis_back_ref)
     image_wait()
-
-
-def arnoldi(first, tables, to_mesh, near_blocks, far_left, far_right, rows, columns, capacity):
+    returned = home(image_back_ref)
+    for s in range(sides):
+        here = lanes[s]
+        next_ref[:, here] = (
+            returned[:, here]
+            - projects[s : s + 1] * mesh_first_ref[:, here]
+            - projects[sides + s : sides + s + 1] * basis_ref[:, here]
+        )
+
+
+def arnoldi(
+    first, tables, to_mesh, to_own, mesh_first, near_blocks, far_left, far_right, rows, columns
+):
     blocks, width = first.shape
     count = rows * columns
     groups = columns
@@ -504,19 +575,22 @@
     pairs = columns // 2
     dma = pltpu.SemaphoreType.DMA
     real, half = jnp.float32, jnp.bfloat16
-    slots = (count, capacity, width)
+    slots = (count, to_mesh.shape[0] // count, width)
     hbm = pl.BlockSpec(memory_space=pl.ANY)
     return pl.pallas_call(
         functools.partial(arnoldi_kernel, rows, columns),
         out_shape=[
-            jax.ShapeDtypeStruct(slots, real),
-            jax.ShapeDtypeStruct(slots, real),
-            jax.ShapeDtypeStruct((2, 8, LANES), real),
+            jax.ShapeDtypeStruct((blocks, width), real),
+            jax.ShapeDtypeStruct((blocks, width), real),
             jax.ShapeDtypeStruct((8, LANES), real),
         ],
-        in_specs=[VMEM] * 3 + [hbm] * 3,
-        out_specs=[VMEM] * 4,
+        in_specs=[VMEM] * 9 + [hbm] * 3,
+        out_specs=[VMEM] * 3,
         scratch_shapes=[
+            pltpu.VMEM((groups, 8, LANES), real),
+            pltpu.VMEM(slots, real),
+            pltpu.VMEM(slots, real),
+            pltpu.VMEM((to_mesh.shape[0], width), real),
             pltpu.VMEM(near_blocks.shape, half),
             pltpu.VMEM(far_left.shape, half),
             pltpu.VMEM(far_right.shape, half),
@@ -540,8 +614,8 @@
             dma((3, groups)),
             dma((2, 2)),
             dma((2, 2)),
-            dma((2, rows)),
-            dma((2, rows)),
+            dma((2, 2, rows - 1)),
+            dma((2, 2, rows - 1)),
             dma((2, pairs)),
             dma((2, pairs)),
             dma((2, pairs)),
@@ -554,7 +628,7 @@
         compiler_params=pltpu.CompilerParams(
             collective_id=1, has_side_effects=True, vmem_limit_bytes=LIMIT
         ),
-    )(first, tables, to_mesh, near_blocks, far_left, far_right)
+    )(first, *tables, to_mesh, to_own, mesh_first, near_blocks, far_left, far_right)
 
 
 def body(
@@ -617,47 +691,28 @@
     first = jnp.dot(to_cluster, arrived[:, :width], precision=HIGH) / norm_lanes[None, :]
 
 
-    group = jnp.arange(columns, dtype=jnp.int32)[:, None]
-
-    def table(values):
-        values = values.reshape(columns, -1)
-        return jnp.pad(values, ((0, 0), (0, lanes - values.shape[1])))
-
-    blank = jnp.zeros((columns, lanes), jnp.int32)
-    tables = jnp.stack(
-        [
-            table(near_columns),
-            table(near_rows),
-            table(far_columns),
-            table(far_rows.reshape(columns, far_count) - group * blocks),
-            table(far_rank),
-            blank,
-            blank,
-            blank,
-        ],
-        axis=1,
-    ).astype(jnp.float32)
+    tables = [
+        values.reshape(columns, -1)
+        for values in (near_columns, near_rows, far_columns, far_rows, far_rank)
+    ]
     to_mesh = (held[:, None] == order[None, :]).astype(jnp.bfloat16)
-    basis_back, image_back, entries, entries_two = arnoldi(
-        first, tables, to_mesh, near_blocks, far_left, far_right, rows, columns, capacity
-    )
-    local = to_slot_f.T
-    project_two = jnp.repeat(entries_two[:sides, 0], lanes)
-    project_three = jnp.repeat(entries_two[sides : 2 * sides, 0], lanes)
-    basis = jnp.dot(local, basis_back.reshape(slots, width), precision=HIGH)
-    image_two = jnp.dot(local, image_back.reshape(slots, width), precision=HIGH)
+    to_own = (slot[:, None] == jnp.arange(slots, dtype=jnp.int32)[None, :]).astype(jnp.bfloat16)
     mesh_first = right_side.reshape(blocks, width) / norm_lanes[None, :]
-    following = image_two - project_two[None, :] * mesh_first - project_three[None, :] * basis
+    basis, following, entries = arnoldi(
+        first,
+        tables,
+        to_mesh,
+        to_own,
+        mesh_first,
+        near_blocks,
+        far_left,
+        far_right,
+        rows,
+        columns,
+    )
     second_basis = basis.reshape(blocks, sides, lanes)
     next_vector = following.reshape(blocks, sides, lanes)
-    hessenberg = jnp.concatenate(
-        [
-            side_norm[None, :],
-            entries[:, :sides, 0],
-            entries_two[: 2 * sides, 0].reshape(2, sides),
-        ],
-        axis=0,
-    )
+    hessenberg = jnp.concatenate([side_norm[None, :], entries[:4, :sides]], axis=0)
     return (second_basis, next_vector, hessenberg)
 
 

time: 157 us -> 153 us (0.975)
  matrix products: 6.25 us -> 3.44 us
    dot_general x2 -> x0, matrix products: 2.81 us -> none  [the longest x1 1.41 us: body(): basis = jnp.dot(local, basis_back.reshape(slots, width), precision=HIGH)]
    slice x3 -> x1, local copies, waits for them, and re-layouts: 2.49 us -> 0.67 us  [body(): entries[:4, :sides]]
where the time goes in v3:
time: 153 us
  Pallas kernels  134 us (88%)
  other arithmetic  7.36 us (5%)
  local copies, waits for them, and re-layouts  6.71 us (4%)
  matrix products  3.44 us (2%)
    pallas_call x1, Pallas kernels, arnoldi(): pl.pallas_call(functools.partial(arnoldi_kernel, rows, columns), out_shap...  114 us
    pallas_call x1, Pallas kernels, exchange(): pl.pallas_call(functools.partial(exchange_kernel, rows, columns), out_sha...  20.6 us

profile of v3, /device:TPU:0, one launch (start us, length us, event | category | flops | bytes accessed | tf_op | source)
XLA Modules:
  0.0 152.6 jit_solution(7624266901528233376)
XLA Ops:
  0.6 0.0 copy-start
  0.6 0.0 copy-start.1
  0.7 0.0 copy-start.2
  0.7 0.7 and_select_fusion.1
  1.4 0.2 convert_reduce_fusion
  1.6 1.3 fusion.1
  2.9 0.1 select_reduce_fusion
  3.0 0.1 broadcast_in_dim.24
  3.1 1.2 multiply_reduce_fusion
  4.3 0.1 broadcast_in_dim.25
  4.4 0.1 reshape.111
  4.5 0.1 pad.4.clone
  4.6 0.9 maximum_bitcast_fusion.send_ref
  5.5 20.6 %shard_map.121 = f32[32,8,640]{2,1,0:T(8,128)} custom-call(f32[32,8,640]{2,1,0:T(8,128)} %maximum_bitcast_fusion.send_ref), custom_call_target="tpu_custom_call" | custom-call | tf_op jit(solution)/shard_map/pallas_call | solution.py:82
  26.1 0.9 convert_add_fusion
  27.0 0.1 copy.20
  27.1 1.0 slice_reduce_fusion
  28.1 0.1 reshape.98
  28.2 0.1 sqrt_reduce_fusion
  28.3 0.1 broadcast_bitcast_fusion
  28.4 2.1 %convolution_divide_fusion.first_ref = f32[128,512]{1,0:T(8,128)} fusion(f32[256,640]{1,0:T(8,128)} %bitcast.24, f32[512]{0:T(512)S(1)} %broadcast_bitcast_fusion, s32[256]{0:T(256)S(1)} %bitcast.29), kind=kOutput, calls=%fused_computation | convolution fusion | flops 201424896 | bytes 789504 | tf_op jit(solution)/shard_map/dot_general | solution.py:691
  30.5 0.0 copy-done
  30.5 0.7 bitcast_divide_fusion.mesh_first_ref
  31.2 0.7 fusion.4.to_mesh_ref
  31.9 0.7 fusion.5.to_own_ref
  32.6 0.0 copy-done.1
  32.6 0.7 reshape.100.near_rows_ref
  33.3 0.0 copy-done.2
  33.3 0.7 reshape.99.near_columns_ref
  34.0 113.8 %shard_map.122 = (f32[128,512]{1,0:T(8,128)}, f32[128,512]{1,0:T(8,128)}, f32[8,128]{1,0:T(8,128)}) custom-call(f32[128,512]{1,0:T(8,128)} %convolution_divide_fusion.first_ref, s32[8,48]{1,0:T(8,128)} %reshape.99.near_columns_ref, s32[8,48]{1,0:T(8,128)} %reshape.100.near_rows_ref, s32[8,128]{1,0:T(8,128)} %bitcast.26, s32[8,128]{1,0:T(8,128)} %bitcast.27, ...), custom_call_target="tpu_custom_call" | custom-call | tf_op jit(solution)/shard_map/pallas_call | solution.py:580
  147.8 0.7 slice.19
  148.4 0.7 copy.17
  149.1 1.7 %reshape.107 = f32[128,4,128]{2,1,0:T(4,128)} reshape(f32[128,512]{1,0:T(8,128)} %get-tuple-element.6) | data formatting | bytes 524288 | tf_op jit(solution)/shard_map/reshape | solution.py:713
  150.9 1.7 %reshape.108 = f32[128,4,128]{2,1,0:T(4,128)} reshape(f32[128,512]{1,0:T(8,128)} %get-tuple-element.7) | data formatting | bytes 524288 | tf_op jit(solution)/shard_map/reshape | solution.py:714
  (3 shorter events, 0.0 us)
Async XLA Ops:
  0.6 29.8 %copy-start = (f32[128,4,128]{2,1,0:T(4,128)S(1)}, f32[128,4,128]{2,1,0:T(4,128)}, u32[]{:S(2)}) copy-start(f32[128,4,128]{2,1,0:T(4,128)} %param.10) | copy-start | bytes 786436
  0.6 32.0 %copy-start.1 = (s32[384]{0:T(512)S(1)}, s32[384]{0:T(512)}, u32[]{:S(2)}) copy-start(s32[384]{0:T(512)} %param.12) | copy-start | bytes 4612
  0.7 32.7 %copy-start.2 = (s32[384]{0:T(512)S(1)}, s32[384]{0:T(512)}, u32[]{:S(2)}) copy-start(s32[384]{0:T(512)} %param.13) | copy-start | bytes 4612
